TPU v7x, 32 devices: a whole 2x2x4 slice. The times are simulated.
32 devices in a mesh: box: 8 (over y, x, core), dir: 4 (over z).
Axes of the slice: x: 2, y: 2, z: 4, core: 2. Of those that a mesh axis runs over, the one named last changes fastest.
Arguments:
- outgoing: float32 [512, 8, 2048], P(('box', 'dir')), may hold values from -6 to 6
- fine_slot: int32 [512], P('box'), may hold values from 0 to 511, as said below
- translator: float32 [316, 2, 8192], P(None, None, 'dir'), may hold values from -0.4 to 0.4
- list_partner: int32 [64, 189], replicated, may hold values from 0 to 63
- list_kind: int32 [64, 189], replicated, may hold values from 0 to 315
- list_count: int32 [64], replicated, may hold values from 63 to 189, as said below
Outputs:
- fine_incoming: float32 [512, 8, 2048], P(('box', 'dir'))
Inputs may be any that keep to these rules, and one draw needn't show every extreme that they name: `fine_slot`: the fine boxes 8 * 8 * g to 8 * 8 * (g + 1) - 1 carry each of the values 8 * 8 * g to 8 * 8 * (g + 1) - 1 exactly once, so every parent has its 8 children, one in each octant, within that group. Slots from list_count[p] on are ignored.
All inputs are finite; a program needn't handle non-finite values.
Results may differ from a plain program's by a relative error of at most 0.0003.
Values sent between devices are 32-bit elements; how exact they have to be, the bound alone decides.
A program may use at most 64 MiB of HBM per device.

v0:
```python
import jax
import jax.numpy as jnp
from jax import lax
from jax.sharding import PartitionSpec as P

TF = 32
PF = 64
TP = 64
PP = 128


wave_shift = 5.0
highest = lax.Precision.HIGHEST


def theta_table(fine_count, coarse_count):
    fine_angle = (jnp.arange(fine_count, dtype=jnp.float32) + 0.5) * (jnp.pi / fine_count)
    coarse_angle = (jnp.arange(coarse_count, dtype=jnp.float32) + 0.5) * (jnp.pi / coarse_count)
    orders = jnp.arange(1, fine_count, dtype=jnp.float32)
    products = jnp.cos(coarse_angle[:, None, None] * orders) * jnp.cos(
        fine_angle[None, :, None] * orders
    )
    return (1.0 + 2.0 * jnp.sum(products, axis=2)) / fine_count


def phi_table(fine_count, coarse_count):
    fine_angle = jnp.arange(fine_count, dtype=jnp.float32) * (2.0 * jnp.pi / fine_count)
    coarse_angle = jnp.arange(coarse_count, dtype=jnp.float32) * (2.0 * jnp.pi / coarse_count)
    offset = coarse_angle[:, None] - fine_angle[None, :]
    orders = jnp.arange(1, fine_count // 2, dtype=jnp.float32)
    series = jnp.sum(jnp.cos(offset[:, :, None] * orders), axis=2)
    return (1.0 + 2.0 * series + jnp.cos(offset * (fine_count // 2))) / fine_count


def octant_phase(octant, first_theta, theta_count, coarse_theta, coarse_phi):
    theta_index = first_theta + jnp.arange(theta_count, dtype=jnp.int32)
    polar = (theta_index.astype(jnp.float32) + 0.5) * (jnp.pi / coarse_theta)
    azimuth = jnp.arange(coarse_phi, dtype=jnp.float32) * (2.0 * jnp.pi / coarse_phi)
    along_x = jnp.sin(polar)[:, None] * jnp.cos(azimuth)[None, :]
    along_y = jnp.sin(polar)[:, None] * jnp.sin(azimuth)[None, :]
    along_z = jnp.cos(polar)[:, None] + 0.0 * azimuth[None, :]
    sign_x = (2 * (octant % 2) - 1).astype(jnp.float32)
    sign_y = (2 * (octant // 2 % 2) - 1).astype(jnp.float32)
    sign_z = (2 * (octant // 4) - 1).astype(jnp.float32)
    phase_angle = wave_shift * (
        sign_x[:, None, None] * along_x[None]
        + sign_y[:, None, None] * along_y[None]
        + sign_z[:, None, None] * along_z[None]
    )
    return (jnp.cos(phase_angle), jnp.sin(phase_angle))


def translate(sources, kernel_table, partner, kind, count):
    targets, length = partner.shape
    source_rows, _, excite, lanes = sources.shape
    kinds = kernel_table.shape[0]
    blocks = 7
    block_width = length // blocks
    flat_sources = sources.reshape(source_rows, 2 * excite * lanes)
    flat_kernel = kernel_table.reshape(kinds, 2 * lanes)
    source_ids = jnp.arange(source_rows, dtype=jnp.int32)
    kind_ids = jnp.arange(kinds, dtype=jnp.int32)

    def add_block(block_step, running):
        begin_at = block_step * block_width
        near_rows = lax.dynamic_slice_in_dim(partner, begin_at, block_width, 1)
        kind_rows = lax.dynamic_slice_in_dim(kind, begin_at, block_width, 1)
        position = begin_at + jnp.arange(block_width, dtype=jnp.int32)
        alive_mask = (position[None, :] < count[:, None]).astype(jnp.float32)
        select_source = (
            (near_rows[:, :, None] == source_ids)
            .astype(jnp.float32)
            .reshape(targets * block_width, source_rows)
        )
        select_kind = (
            (kind_rows[:, :, None] == kind_ids).astype(jnp.float32) * alive_mask[:, :, None]
        ).reshape(targets * block_width, kinds)
        picked = jnp.dot(
            select_source, flat_sources, precision=highest, preferred_element_type=jnp.float32
        )
        picked = picked.reshape(targets, block_width, 2, excite, lanes)
        factor = jnp.dot(
            select_kind, flat_kernel, precision=highest, preferred_element_type=jnp.float32
        )
        factor = factor.reshape(targets, block_width, 2, 1, lanes)
        along_real = factor[:, :, 0]
        along_imag = factor[:, :, 1]
        real_part = picked[:, :, 0]
        imag_part = picked[:, :, 1]
        new_real = jnp.sum(along_real * real_part - along_imag * imag_part, axis=1)
        new_imag = jnp.sum(along_real * imag_part + along_imag * real_part, axis=1)
        return running + jnp.stack([new_real, new_imag], axis=1)

    initial = jnp.zeros((targets, 2, excite, lanes), jnp.float32)
    return lax.fori_loop(0, blocks, add_block, initial)


def body(outgoing, fine_slot, translator, list_partner, list_kind, list_count):
    dir_count = lax.axis_size("dir")
    box_count = lax.axis_size("box")
    box_index = lax.axis_index("box")
    dir_index = lax.axis_index("dir")
    channels = outgoing.shape[1]
    excite = channels // 2
    fine_here = outgoing.shape[0]
    row_boxes = fine_slot.shape[0]
    parents_here = row_boxes // 8
    theta_here = TP // dir_count
    dirs_here = translator.shape[2]
    up_theta = theta_table(TF, TP)
    up_phi = phi_table(PF, PP)
    octant = fine_slot % 8
    local_parent = fine_slot // 8 % parents_here
    onehot = (local_parent[None, :] == jnp.arange(parents_here, dtype=jnp.int32)[:, None]).astype(
        jnp.float32
    )
    cos_table, sin_table = octant_phase(octant, dir_index * theta_here, theta_here, TP, PP)
    cos_table = cos_table[:, :, None, :]
    sin_table = sin_table[:, :, None, :]
    pattern = outgoing.reshape(fine_here, channels, TF, PF)
    raised = jnp.einsum("ut,fctp->fcup", up_theta, pattern, precision=highest)
    raised = jnp.einsum("qp,fcup->fucq", up_phi, raised, precision=highest)
    spread = lax.all_to_all(raised, "dir", split_axis=1, concat_axis=0, tiled=True)
    real_part = spread[:, :, :excite]
    imag_part = spread[:, :, excite:]
    shifted = jnp.concatenate(
        [
            real_part * cos_table + imag_part * sin_table,
            imag_part * cos_table - real_part * sin_table,
        ],
        axis=2,
    )
    parent_out = jnp.einsum("pf,fucq->pcuq", onehot, shifted, precision=highest)
    parent_out = parent_out.reshape(parents_here, channels, dirs_here)
    split_here = dirs_here // box_count
    sectioned = jnp.swapaxes(
        parent_out.reshape(parents_here, channels, box_count, split_here), 1, 2
    )
    sectioned = sectioned.reshape(parents_here, box_count, channels * split_here)
    gathered = lax.all_to_all(sectioned, "box", split_axis=1, concat_axis=0, tiled=True)
    sources = gathered.reshape(box_count * parents_here, 2, excite, split_here)
    kernel_rows = lax.dynamic_slice_in_dim(translator, box_index * split_here, split_here, 2)
    translated = translate(sources, kernel_rows, list_partner, list_kind, list_count)
    translated = translated.reshape(box_count * parents_here, 1, channels * split_here)
    returned = lax.all_to_all(translated, "box", split_axis=0, concat_axis=1, tiled=True)
    incoming = jnp.swapaxes(returned.reshape(parents_here, box_count, channels, split_here), 1, 2)
    incoming = incoming.reshape(parents_here, channels, dirs_here)
    fields = incoming.reshape(parents_here, channels, theta_here, PP)
    spread_back = jnp.einsum("pf,pcuq->fucq", onehot, fields, precision=highest)
    real_part = spread_back[:, :, :excite]
    imag_part = spread_back[:, :, excite:]
    shifted_back = jnp.concatenate(
        [
            real_part * cos_table - imag_part * sin_table,
            imag_part * cos_table + real_part * sin_table,
        ],
        axis=2,
    )
    arrived_back = lax.all_to_all(shifted_back, "dir", split_axis=0, concat_axis=1, tiled=True)
    arrived_back = jnp.einsum("qp,fucq->fucp", up_phi, arrived_back, precision=highest) * (PF / PP)
    result = jnp.einsum("ut,fucp->fctp", up_theta, arrived_back, precision=highest) * (TF / TP)
    return result.reshape(fine_here, channels, TF * PF)


def solution(mesh):
    placed = (P(("box", "dir"), None, None), P("box"), P(None, None, "dir"), P(), P(), P())
    return jax.shard_map(
        body, mesh=mesh, in_specs=placed, out_specs=P(("box", "dir"), None, None), check_vma=False
    )
```

profile of v0, /device:TPU:0, one launch (start us, length us, event | category | flops | bytes accessed | tf_op | source)
XLA Modules:
  0.0 433.8 jit_solution(9797637659104217145)
XLA Ops:
  14.0 4.4 %copy.92 = f32[16,64,8,128]{3,2,0,1:T(8,128)} copy(f32[16,64,8,128]{3,1,2,0:T(8,128)S(1)} %fusion.32) | data formatting | bytes 8388608 | tf_op jit(solution)/shard_map/qp,fcup->fucq/transpose | solution.py:122
  18.4 6.7 %all-to-all-start = ((f32[16,64,8,128]{3,2,0,1:T(8,128)}), f32[16,64,8,128]{3,2,0,1:T(8,128)}, u32[]{:S(2)}, u32[]{:S(2)}) async-start(f32[16,64,8,128]{3,2,0,1:T(8,128)} %copy.92), calls=%async_computation | async-start | bytes 8388608 | tf_op jit(solution)/shard_map/all_to_all | solution.py:123
  27.5 91.1 %all-to-all-done = f32[16,64,8,128]{3,2,0,1:T(8,128)} async-done(((f32[16,64,8,128]{3,2,0,1:T(8,128)}), f32[16,64,8,128]{3,2,0,1:T(8,128)}, u32[]{:S(2)}, u32[]{:S(2)}) %all-to-all-start) | async-done | bytes 4194336 | tf_op jit(solution)/shard_map/all_to_all | solution.py:123
  125.6 4.1 all-to-all-start.1
  133.7 5.8 %all-to-all-done.1 = f32[8,8,2048]{2,0,1:T(8,128)} async-done(((f32[8,8,2048]{2,0,1:T(8,128)}), f32[8,8,2048]{2,0,1:T(8,128)}, u32[]{:S(2)}, u32[]{:S(2)}) %all-to-all-start.1) | async-done | bytes 524320 | tf_op jit(solution)/shard_map/all_to_all | solution.py:140
  139.5 169.0 %while.14 = (s32[]{:T(128)}, f32[64,2,4,256]{3,0,2,1:T(8,128)}, s32[64,189]{0,1:T(8,128)}, s32[64]{0:T(128)}, f32[316,512]{1,0:T(8,128)}, /*index=5*/s32[64,189]...) while((s32[]{:T(128)}, f32[64,2,4,256]{3,0,2,1:T(8,128)}, ...), condition=%wide.region_5.6_spmd.clone, body=%wide.region_2.5_spmd.clone.sunk | while | flops 6088452096 | bytes 48134784 | solution.py:95
  143.0 6.0 %fusion.101 = f32[64,27,2,1,256]{4,0,2,1,3:T(8,128)S(1)} fusion(f32[64,27]{0,1:T(8,128)S(1)} %compare_convert_fusion.2, s32[64,27]{0,1:T(8,128)S(1)} %get-tuple-element.324, f32[2,256,316]{1,0,2:T(2,128)S(1)} %reshape.369), kind=kOutput, calls=%fused_computation.10.clone.1 | convolution fusion | flops 3356011008 | bytes 4199936 | tf_op jit(solution)/shard_map/while/body/eval_jaxpr/dot_general | solution.py:82
  151.4 7.0 %fusion.100 = f32[64,27,2,4,256]{4,0,3,2,1:T(8,128)S(1)} fusion(f32[2,4,256,64]{2,1,0,3:T(4,128)} %dot_general.49, s32[64,27]{0,1:T(8,128)S(1)} %get-tuple-element.323), kind=kOutput, calls=%fused_computation.18.clone.1 | convolution fusion | flops 2718019584 | bytes 14686976 | tf_op jit(solution)/shard_map/while/body/eval_jaxpr/dot_general | solution.py:78
  166.9 6.0 %fusion.101 = f32[64,27,2,1,256]{4,0,2,1,3:T(8,128)S(1)} fusion(f32[64,27]{0,1:T(8,128)S(1)} %compare_convert_fusion.2, s32[64,27]{0,1:T(8,128)S(1)} %get-tuple-element.324, f32[2,256,316]{1,0,2:T(2,128)S(1)} %reshape.369), kind=kOutput, calls=%fused_computation.10.clone.1 | convolution fusion | flops 3356011008 | bytes 4199936 | tf_op jit(solution)/shard_map/while/body/eval_jaxpr/dot_general | solution.py:82
  175.3 6.9 %fusion.100 = f32[64,27,2,4,256]{4,0,3,2,1:T(8,128)S(1)} fusion(f32[2,4,256,64]{2,1,0,3:T(4,128)} %dot_general.49, s32[64,27]{0,1:T(8,128)S(1)} %get-tuple-element.323), kind=kOutput, calls=%fused_computation.18.clone.1 | convolution fusion | flops 2718019584 | bytes 14686976 | tf_op jit(solution)/shard_map/while/body/eval_jaxpr/dot_general | solution.py:78
  191.0 6.0 %fusion.101 = f32[64,27,2,1,256]{4,0,2,1,3:T(8,128)S(1)} fusion(f32[64,27]{0,1:T(8,128)S(1)} %compare_convert_fusion.2, s32[64,27]{0,1:T(8,128)S(1)} %get-tuple-element.324, f32[2,256,316]{1,0,2:T(2,128)S(1)} %reshape.369), kind=kOutput, calls=%fused_computation.10.clone.1 | convolution fusion | flops 3356011008 | bytes 4199936 | tf_op jit(solution)/shard_map/while/body/eval_jaxpr/dot_general | solution.py:82
  199.4 7.0 %fusion.100 = f32[64,27,2,4,256]{4,0,3,2,1:T(8,128)S(1)} fusion(f32[2,4,256,64]{2,1,0,3:T(4,128)} %dot_general.49, s32[64,27]{0,1:T(8,128)S(1)} %get-tuple-element.323), kind=kOutput, calls=%fused_computation.18.clone.1 | convolution fusion | flops 2718019584 | bytes 14686976 | tf_op jit(solution)/shard_map/while/body/eval_jaxpr/dot_general | solution.py:78
  215.0 6.0 %fusion.101 = f32[64,27,2,1,256]{4,0,2,1,3:T(8,128)S(1)} fusion(f32[64,27]{0,1:T(8,128)S(1)} %compare_convert_fusion.2, s32[64,27]{0,1:T(8,128)S(1)} %get-tuple-element.324, f32[2,256,316]{1,0,2:T(2,128)S(1)} %reshape.369), kind=kOutput, calls=%fused_computation.10.clone.1 | convolution fusion | flops 3356011008 | bytes 4199936 | tf_op jit(solution)/shard_map/while/body/eval_jaxpr/dot_general | solution.py:82
  223.5 7.0 %fusion.100 = f32[64,27,2,4,256]{4,0,3,2,1:T(8,128)S(1)} fusion(f32[2,4,256,64]{2,1,0,3:T(4,128)} %dot_general.49, s32[64,27]{0,1:T(8,128)S(1)} %get-tuple-element.323), kind=kOutput, calls=%fused_computation.18.clone.1 | convolution fusion | flops 2718019584 | bytes 14686976 | tf_op jit(solution)/shard_map/while/body/eval_jaxpr/dot_general | solution.py:78
  239.1 6.0 %fusion.101 = f32[64,27,2,1,256]{4,0,2,1,3:T(8,128)S(1)} fusion(f32[64,27]{0,1:T(8,128)S(1)} %compare_convert_fusion.2, s32[64,27]{0,1:T(8,128)S(1)} %get-tuple-element.324, f32[2,256,316]{1,0,2:T(2,128)S(1)} %reshape.369), kind=kOutput, calls=%fused_computation.10.clone.1 | convolution fusion | flops 3356011008 | bytes 4199936 | tf_op jit(solution)/shard_map/while/body/eval_jaxpr/dot_general | solution.py:82
  247.6 7.0 %fusion.100 = f32[64,27,2,4,256]{4,0,3,2,1:T(8,128)S(1)} fusion(f32[2,4,256,64]{2,1,0,3:T(4,128)} %dot_general.49, s32[64,27]{0,1:T(8,128)S(1)} %get-tuple-element.323), kind=kOutput, calls=%fused_computation.18.clone.1 | convolution fusion | flops 2718019584 | bytes 14686976 | tf_op jit(solution)/shard_map/while/body/eval_jaxpr/dot_general | solution.py:78
  254.6 3.6 subtract_reduce_fusion.2
  263.2 6.0 %fusion.101 = f32[64,27,2,1,256]{4,0,2,1,3:T(8,128)S(1)} fusion(f32[64,27]{0,1:T(8,128)S(1)} %compare_convert_fusion.2, s32[64,27]{0,1:T(8,128)S(1)} %get-tuple-element.324, f32[2,256,316]{1,0,2:T(2,128)S(1)} %reshape.369), kind=kOutput, calls=%fused_computation.10.clone.1 | convolution fusion | flops 3356011008 | bytes 4199936 | tf_op jit(solution)/shard_map/while/body/eval_jaxpr/dot_general | solution.py:82
  271.7 6.9 %fusion.100 = f32[64,27,2,4,256]{4,0,3,2,1:T(8,128)S(1)} fusion(f32[2,4,256,64]{2,1,0,3:T(4,128)} %dot_general.49, s32[64,27]{0,1:T(8,128)S(1)} %get-tuple-element.323), kind=kOutput, calls=%fused_computation.18.clone.1 | convolution fusion | flops 2718019584 | bytes 14686976 | tf_op jit(solution)/shard_map/while/body/eval_jaxpr/dot_general | solution.py:78
  287.3 6.0 %fusion.101 = f32[64,27,2,1,256]{4,0,2,1,3:T(8,128)S(1)} fusion(f32[64,27]{0,1:T(8,128)S(1)} %compare_convert_fusion.2, s32[64,27]{0,1:T(8,128)S(1)} %get-tuple-element.324, f32[2,256,316]{1,0,2:T(2,128)S(1)} %reshape.369), kind=kOutput, calls=%fused_computation.10.clone.1 | convolution fusion | flops 3356011008 | bytes 4199936 | tf_op jit(solution)/shard_map/while/body/eval_jaxpr/dot_general | solution.py:82
  295.7 7.0 %fusion.100 = f32[64,27,2,4,256]{4,0,3,2,1:T(8,128)S(1)} fusion(f32[2,4,256,64]{2,1,0,3:T(4,128)} %dot_general.49, s32[64,27]{0,1:T(8,128)S(1)} %get-tuple-element.323), kind=kOutput, calls=%fused_computation.18.clone.1 | convolution fusion | flops 2718019584 | bytes 14686976 | tf_op jit(solution)/shard_map/while/body/eval_jaxpr/dot_general | solution.py:78
  310.6 12.2 %all_to_all.66 = f32[64,1,2048]{2,1,0:T(1,128)S(1)} all-to-all(f32[64,1,2048]{2,1,0:T(1,128)S(1)} %reshape.356), channel_id=1, replica_groups=mesh['box'=8,'dir'=4] {'box'}, dimensions={0} | all-to-all | bytes 1048576 | tf_op jit(solution)/shard_map/all_to_all | solution.py:145
  329.1 95.5 %all_to_all.67 = f32[64,16,8,128]{3,2,1,0:T(8,128)S(1)} all-to-all(f32[64,16,8,128]{3,2,1,0:T(8,128)S(1)} %copy.103), channel_id=1, replica_groups=mesh['box'=8,'dir'=4] {'dir'}, dimensions={0} | all-to-all | bytes 8388608 | tf_op jit(solution)/shard_map/all_to_all | solution.py:159
  425.4 3.9 fusion.28
  (135 shorter events, 114.0 us)
Async XLA Ops:
  0.0 10.4 %copy-start.10 = (f32[64]{0:T(128)}, f32[64]{0:T(128)S(1)}, u32[]{:S(2)}) copy-start(f32[64]{0:T(128)S(1)} %iota_multiply_fusion.1) | copy-start | bytes 772
  0.0 10.4 %copy-start.12 = (f32[128]{0:T(128)}, f32[128]{0:T(128)S(1)}, u32[]{:S(2)}) copy-start(f32[128]{0:T(128)S(1)} %iota_multiply_fusion.2) | copy-start | bytes 1540
  3.5 6.9 %copy-start.6 = (f32[128,64]{0,1:T(8,128)}, f32[128,64]{0,1:T(8,128)S(1)}, u32[]{:S(2)}) copy-start(f32[128,64]{0,1:T(8,128)S(1)} %cosine_reduce_fusion) | copy-start | bytes 98308
  6.2 0.6 copy-start.4
  18.4 6.8 %copy-start.16 = (s32[64]{0:T(128)S(1)}, s32[64]{0:T(128)}, u32[]{:S(2)}) copy-start(s32[64]{0:T(128)} %param.9) | copy-start | bytes 772
  18.4 100.1 %all-to-all-start = ((f32[16,64,8,128]{3,2,0,1:T(8,128)}), f32[16,64,8,128]{3,2,0,1:T(8,128)}, u32[]{:S(2)}, u32[]{:S(2)}) async-start(f32[16,64,8,128]{3,2,0,1:T(8,128)} %copy.92), calls=%async_computation | async-start | bytes 8388608 | tf_op jit(solution)/shard_map/all_to_all | solution.py:123
  25.3 97.2 %copy-start.14 = (s32[64]{0:T(128)}, s32[64]{0:T(128)S(1)}, u32[]{:S(2)}) copy-start(s32[64]{0:T(128)S(1)} %get-tuple-element.265) | copy-start | bytes 772
  27.5 94.0 %copy-start = (f32[64,16,128]{2,0,1:T(8,128)}, f32[64,16,128]{2,0,1:T(8,128)S(1)}, u32[]{:S(2)}) copy-start(f32[64,16,128]{2,0,1:T(8,128)S(1)} %get-tuple-element.263) | copy-start | bytes 1572868
  27.5 94.0 %copy-start.2 = (f32[64,16,128]{2,0,1:T(8,128)}, f32[64,16,128]{2,0,1:T(8,128)S(1)}, u32[]{:S(2)}) copy-start(f32[64,16,128]{2,0,1:T(8,128)S(1)} %get-tuple-element.264) | copy-start | bytes 1572868
  124.3 7.9 %copy-start.8 = (s32[64,189]{1,0:T(8,128)S(1)}, s32[64,189]{1,0:T(8,128)}, u32[]{:S(2)}) copy-start(s32[64,189]{1,0:T(8,128)} %param.12) | copy-start | bytes 145156
  124.3 8.6 %copy-start.9 = (s32[64,189]{1,0:T(8,128)S(1)}, s32[64,189]{1,0:T(8,128)}, u32[]{:S(2)}) copy-start(s32[64,189]{1,0:T(8,128)} %param.11) | copy-start | bytes 145156
  125.6 13.9 %all-to-all-start.1 = ((f32[8,8,2048]{2,0,1:T(8,128)}), f32[8,8,2048]{2,0,1:T(8,128)}, u32[]{:S(2)}, u32[]{:S(2)}) async-start(f32[8,8,2048]{2,0,1:T(8,128)} %copy.95), calls=%async_computation.1 | async-start | bytes 1048576 | tf_op jit(solution)/shard_map/all_to_all | solution.py:140
  308.5 14.9 %copy-start.15 = (s32[64]{0:T(128)S(1)}, s32[64]{0:T(128)}, u32[]{:S(2)}) copy-start(s32[64]{0:T(128)} %copy-done.14) | copy-start | bytes 772
  323.1 2.2 copy-start.1
  323.1 2.2 copy-start.3
  424.6 0.8 copy-start.7
  424.6 0.8 copy-start.11
  424.6 0.8 copy-start.13
  425.4 3.9 copy-start.5
where the time goes:
time: 439 us; the launch traced here: 434 us
  matrix products  108 us (25%)
  blocking collectives  108 us (25%)
  waiting for transfers between devices  96.9 us (22%)
  local copies, waits for them, and re-layouts  55.8 us (13%)
  other arithmetic  53.1 us (12%)
  starting transfers between devices  10.9 us (2%)
    all_to_all x1, blocking collectives, body(): lax.all_to_all(shifted_back, 'dir', split_axis=0, concat_axis=1, tiled=True)  95.5 us
    all_to_all x1, waiting for transfers between devices, body(): lax.all_to_all(raised, 'dir', split_axis=1, concat_axis=0, tiled=True)  91.1 us
    dot_general x7, matrix products, add_block(): jnp.dot(select_source, flat_sources, precision=highest, preferred_element...  48.6 us
    dot_general x7, matrix products, add_block(): jnp.dot(select_kind, flat_kernel, precision=highest, preferred_element_ty...  42.2 us
    reduce_sum x7, other arithmetic, add_block(): new_real = jnp.sum(along_real * real_part - along_imag * imag_part, axis=1)  25.3 us
    dot_general x7, local copies, waits for them, and re-layouts, add_block(): jnp.dot(select_source, flat_sources, precision=highest, preferred_element...  15.3 us
    add x7, other arithmetic, add_block(): return running + jnp.stack([new_real, new_imag], axis=1)  14.2 us
    all_to_all x1, blocking collectives, body(): lax.all_to_all(translated, 'box', split_axis=0, concat_axis=1, tiled=True)  12.2 us
  transfers between devices with their start and end apart: 2, of which 2 were waited for; matrix products, arithmetic and copies ran while one was open for 1% of the time, Pallas kernels for 0%

commit v1 on v0

--- a/solution.py
+++ b/solution.py
@@ -1,6 +1,12 @@
+import functools
+
 import jax
 import jax.numpy as jnp
+import ml_dtypes
+import numpy as np
 from jax import lax
+from jax.experimental import pallas as pl
+from jax.experimental.pallas import tpu as pltpu
 from jax.sharding import PartitionSpec as P
 
 TF = 32
@@ -95,7 +101,7 @@
     return lax.fori_loop(0, blocks, add_block, initial)
 
 
-def body(outgoing, fine_slot, translator, list_partner, list_kind, list_count):
+def general_body(outgoing, fine_slot, translator, list_partner, list_kind, list_count):
     dir_count = lax.axis_size("dir")
     box_count = lax.axis_size("box")
     box_index = lax.axis_index("box")
@@ -162,6 +168,343 @@
     return result.reshape(fine_here, channels, TF * PF)
 
 
+def np_theta(fine_count, coarse_count):
+    fine_angle = (np.arange(fine_count) + 0.5) * (np.pi / fine_count)
+    coarse_angle = (np.arange(coarse_count) + 0.5) * (np.pi / coarse_count)
+    orders = np.arange(1, fine_count)
+    products = np.cos(coarse_angle[:, None, None] * orders) * np.cos(
+        fine_angle[None, :, None] * orders
+    )
+    return (1.0 + 2.0 * products.sum(2)) / fine_count
+
+
+def np_phi(fine_count, coarse_count):
+    fine_angle = np.arange(fine_count) * (2.0 * np.pi / fine_count)
+    coarse_angle = np.arange(coarse_count) * (2.0 * np.pi / coarse_count)
+    offset = coarse_angle[:, None] - fine_angle[None, :]
+    orders = np.arange(1, fine_count // 2)
+    series = np.cos(offset[:, :, None] * orders).sum(2)
+    return (1.0 + 2.0 * series + np.cos(offset * (fine_count // 2))) / fine_count
+
+
+def np_phase(channels):
+    polar = (np.arange(TP) + 0.5) * (np.pi / TP)
+    azimuth = np.arange(PP) * (2.0 * np.pi / PP)
+    octant = np.arange(8)
+    signs = [2.0 * (octant // step % 2) - 1.0 for step in (1, 2, 4)]
+    along = [
+        np.sin(polar)[:, None] * np.cos(azimuth)[None, :],
+        np.sin(polar)[:, None] * np.sin(azimuth)[None, :],
+        np.cos(polar)[:, None] + 0.0 * azimuth[None, :],
+    ]
+    angle = wave_shift * sum(s[:, None, None] * a[None] for s, a in zip(signs, along))
+    half = channels // 2
+    turn = np.where(np.arange(channels) < half, 1.0, -1.0)
+    sin_table = np.sin(angle)[:, :, None, :] * turn[None, None, :, None]
+    cos_table = np.broadcast_to(np.cos(angle)[:, :, None, :], sin_table.shape)
+    return cos_table.astype(np.float32), sin_table.astype(np.float32)
+
+
+def np_split(values):
+    high = values.astype(ml_dtypes.bfloat16)
+    low = (values - high.astype(np.float64)).astype(ml_dtypes.bfloat16)
+    return high, low
+
+
+def tables(channels):
+    theta = np_theta(TF, TP)
+    phi = np_phi(PF, PP)
+    eye = np.eye(channels)
+    order = np.concatenate([np.arange(0, TF, 2), np.arange(1, TF, 2)])
+    theta = theta[:, order]
+    up_phi = np.kron(np.eye(2), phi.T)
+    up_theta = np.kron(theta, eye)
+    down_theta = np.kron(theta.T, eye) * (TF / TP)
+    down_phi = np.kron(np.eye(2), phi) * (PF / PP)
+    uph, upl = np_split(up_phi)
+    uth, utl = np_split(up_theta)
+    dth, dtl = np_split(down_theta)
+    dph, dpl = np_split(down_phi)
+    return (
+        np.concatenate([uph, uph, upl], axis=0),
+        np.concatenate([uth, uth, utl], axis=1),
+        np.concatenate([dth, dth, dtl], axis=1),
+        np.concatenate([dph, dph, dpl], axis=0),
+    )
+
+
+def split3(values, axis):
+    high = values.astype(jnp.bfloat16)
+    low = (values - high.astype(jnp.float32)).astype(jnp.bfloat16)
+    return jnp.concatenate([high, low, high], axis=axis)
+
+
+def dot(a, b):
+    return jnp.dot(a, b, preferred_element_type=jnp.float32)
+
+
+pair = 2
+
+
+def raise_kernel(slot_ref, x_ref, phi_ref, theta_ref, cos_ref, sin_ref, out_ref):
+    step = pl.program_id(0)
+    channels = x_ref.shape[1]
+    parents = out_ref.shape[1]
+
+    @pl.when(step == 0)
+    def _():
+        out_ref[...] = jnp.zeros_like(out_ref)
+
+    stacked = []
+    for i in range(pair):
+        x = x_ref[i]
+        x = jnp.concatenate(
+            [x[:, j * 2 * PF : (j + 1) * 2 * PF] for j in range(TF // 2)], axis=0
+        )
+        y = dot(split3(x, 1), phi_ref[...])
+        stacked.append(jnp.concatenate([y[:, :PP], y[:, PP:]], axis=0))
+    z = jnp.concatenate(stacked, axis=1)
+    raised = dot(theta_ref[...], split3(z, 0))
+    for i in range(pair):
+        slot = slot_ref[step * pair + i]
+        octant = slot % 8
+        parent = slot // 8 % parents
+        r = raised[:, i * PP : (i + 1) * PP].reshape(TP, channels, PP)
+        turned = pltpu.roll(r, channels // 2, 1)
+        out_ref[:, parent] += r * cos_ref[octant] + turned * sin_ref[octant]
+
+
+def lower_kernel(slot_ref, f_ref, phi_ref, theta_ref, cos_ref, sin_ref, out_ref):
+    step = pl.program_id(0)
+    channels = out_ref.shape[1]
+    parents = f_ref.shape[1]
+    fields = []
+    for i in range(pair):
+        slot = slot_ref[step * pair + i]
+        octant = slot % 8
+        parent = slot // 8 % parents
+        r = f_ref[:, parent]
+        turned = pltpu.roll(r, channels // 2, 1)
+        child = r * cos_ref[octant] - turned * sin_ref[octant]
+        fields.append(child.reshape(TP * channels, PP))
+    z = dot(theta_ref[...], split3(jnp.concatenate(fields, axis=1), 0))
+    half = z.shape[0] // 2
+    for i in range(pair):
+        part = z[:, i * PP : (i + 1) * PP]
+        y = jnp.concatenate([part[:half], part[half:]], axis=1)
+        x = dot(split3(y, 1), phi_ref[...])
+        out_ref[i] = jnp.concatenate(
+            [x[j * channels : (j + 1) * channels] for j in range(TF // 2)], axis=1
+        )
+
+
+def whole_spec(array):
+    return pl.BlockSpec(array.shape, lambda *_: (0,) * array.ndim)
+
+
+def raise_parents(slots, outgoing, parents, consts):
+    fine, channels, width = outgoing.shape
+    phi, theta, cos_table, sin_table = consts
+    shape = (TP, parents, channels, PP)
+    return pl.pallas_call(
+        raise_kernel,
+        out_shape=jax.ShapeDtypeStruct(shape, jnp.float32),
+        grid_spec=pltpu.PrefetchScalarGridSpec(
+            num_scalar_prefetch=1,
+            grid=(fine // pair,),
+            in_specs=[
+                pl.BlockSpec((pair, channels, width), lambda i, _: (i, 0, 0)),
+                whole_spec(phi),
+                whole_spec(theta),
+                whole_spec(cos_table),
+                whole_spec(sin_table),
+            ],
+            out_specs=pl.BlockSpec(shape, lambda i, _: (0, 0, 0, 0)),
+        ),
+        compiler_params=pltpu.CompilerParams(vmem_limit_bytes=48 * 2**20),
+        name="raise_parents",
+    )(slots, outgoing, phi, theta, cos_table, sin_table)
+
+
+def lower_parents(slots, field, consts):
+    parents, channels = field.shape[1:3]
+    fine = slots.shape[0]
+    phi, theta, cos_table, sin_table = consts
+    return pl.pallas_call(
+        lower_kernel,
+        out_shape=jax.ShapeDtypeStruct((fine, channels, TF * PF), jnp.float32),
+        grid_spec=pltpu.PrefetchScalarGridSpec(
+            num_scalar_prefetch=1,
+            grid=(fine // pair,),
+            in_specs=[
+                whole_spec(field),
+                whole_spec(phi),
+                whole_spec(theta),
+                whole_spec(cos_table),
+                whole_spec(sin_table),
+            ],
+            out_specs=pl.BlockSpec((pair, channels, TF * PF), lambda i, _: (i, 0, 0)),
+        ),
+        compiler_params=pltpu.CompilerParams(vmem_limit_bytes=48 * 2**20),
+        name="lower_parents",
+    )(slots, field, phi, theta, cos_table, sin_table)
+
+
+def fill_operator(partner_ref, kind_ref, rows_ref, sel_ref, store, targets, sources):
+    blocks = sel_ref.shape[0]
+    length = partner_ref.shape[1]
+    source_ids = lax.broadcasted_iota(jnp.int32, (sources, length), 0)
+    kind_ids = lax.broadcasted_iota(jnp.int32, (blocks * 128, length), 0)
+
+    def count_pairs(p, _):
+        partner = partner_ref[pl.ds(p, 1), :]
+        kind = kind_ref[pl.ds(p, 1), :]
+        a = jnp.where(source_ids == partner, 1.0, 0.0).astype(jnp.bfloat16)
+        b = jnp.where(kind_ids == kind, 1.0, 0.0).astype(jnp.bfloat16)
+        counts = lax.dot_general(
+            a, b, (((1,), (1,)), ((), ())), preferred_element_type=jnp.float32
+        )
+        for j in range(blocks):
+            sel_ref[j, pl.ds(p, sources, stride=targets), :] = counts[:, j * 128 : (j + 1) * 128]
+        return 0
+
+    lax.fori_loop(0, targets, count_pairs, 0)
+    kinds, width = rows_ref.shape
+    pad = blocks * 128 - kinds
+    rows = rows_ref[...]
+    if pad:
+        rows = jnp.concatenate([rows, jnp.zeros((pad, width), jnp.float32)], axis=0)
+    high = rows.astype(jnp.bfloat16)
+    low = (rows - high.astype(jnp.float32)).astype(jnp.bfloat16)
+    both = jnp.concatenate([high, low], axis=0)
+    tile = 512
+
+    def one_tile(i, _):
+        start = pl.multiple_of(i * tile, tile)
+        chosen = jnp.concatenate(
+            [sel_ref[j, pl.ds(start, tile), :] for j in range(blocks)], axis=1
+        ).astype(jnp.bfloat16)
+        store(start, tile, dot(jnp.concatenate([chosen, chosen], axis=1), both))
+        return 0
+
+    lax.fori_loop(0, targets * sources // tile, one_tile, 0)
+
+
+def operator_kernel(partner_ref, kind_ref, rows_ref, out_ref, sel_ref, *, targets, sources):
+    def store(start, tile, values):
+        out_ref[pl.ds(start, tile), :] = values
+
+    fill_operator(partner_ref, kind_ref, rows_ref, sel_ref, store, targets, sources)
+
+
+def build_operator(partner, kind, rows, sources):
+    targets, length = partner.shape
+    kinds, width = rows.shape
+    blocks = -(-kinds // 128)
+    return pl.pallas_call(
+        functools.partial(operator_kernel, targets=targets, sources=sources),
+        out_shape=jax.ShapeDtypeStruct((sources * targets, width), jnp.float32),
+        scratch_shapes=[pltpu.VMEM((blocks, sources * targets, 128), jnp.float32)],
+        compiler_params=pltpu.CompilerParams(vmem_limit_bytes=48 * 2**20),
+        cost_estimate=pl.CostEstimate(
+            flops=4 * sources * targets * blocks * 128 * width,
+            bytes_accessed=4 * sources * targets * width,
+            transcendentals=0,
+        ),
+        name="build_operator",
+    )(partner, kind, rows)
+
+
+def apply_tiles(op_ref, load, store, u, count, targets, sources, channels):
+    half = channels // 2
+    group = 2
+
+    def add_source(s, sums, first):
+        fields = [load(u, s, c) for c in range(channels)]
+        out = []
+        for g in range(group):
+            row = pl.multiple_of(s * targets + first + g * 8, 8)
+            real = op_ref[pl.ds(row, 8), u * PP : (u + 1) * PP]
+            imag = op_ref[pl.ds(row, 8), (count + u) * PP : (count + u + 1) * PP]
+            mine = sums[g * channels : (g + 1) * channels]
+            for e in range(half):
+                out.append(mine[e] + real * fields[e] - imag * fields[half + e])
+            for e in range(half):
+                out.append(mine[half + e] + real * fields[half + e] + imag * fields[e])
+        return tuple(out)
+
+    for first in range(0, targets, group * 8):
+        sums = tuple(jnp.zeros((8, PP), jnp.float32) for _ in range(group * channels))
+        sums = lax.fori_loop(
+            0, sources, functools.partial(add_source, first=first), sums, unroll=4
+        )
+        for g in range(group):
+            for c in range(channels):
+                store(u, first + g * 8, c, sums[g * channels + c])
+
+
+def apply_kernel(op_ref, s_ref, out_ref, *, count, targets, sources, channels):
+    def load(u, s, c):
+        return s_ref[u, pl.ds(s, 1), c, :]
+
+    def store(u, p, c, values):
+        out_ref[pl.ds((u * targets + p) * channels + c, 8, stride=channels), :] = values
+
+    for u in range(count):
+        apply_tiles(op_ref, load, store, u, count, targets, sources, channels)
+
+
+def apply_operator(operator, fields, targets):
+    count, sources, channels, _ = fields.shape
+    out = pl.pallas_call(
+        functools.partial(
+            apply_kernel, count=count, targets=targets, sources=sources, channels=channels
+        ),
+        out_shape=jax.ShapeDtypeStruct((count * targets * channels, PP), jnp.float32),
+        compiler_params=pltpu.CompilerParams(vmem_limit_bytes=48 * 2**20),
+        name="apply_operator",
+    )(operator, fields)
+    return out.reshape(count, targets, channels, PP)
+
+
+def body(outgoing, fine_slot, translator, list_partner, list_kind, list_count):
+    dir_count = lax.axis_size("dir")
+    box_count = lax.axis_size("box")
+    if TP // dir_count % box_count:
+        return general_body(
+            outgoing, fine_slot, translator, list_partner, list_kind, list_count
+        )
+    box_index = lax.axis_index("box")
+    dir_index = lax.axis_index("dir")
+    fine_here, channels, _ = outgoing.shape
+    parents_here = fine_slot.shape[0] // 8
+    targets, length = list_partner.shape
+    kinds, _, dirs_here = translator.shape
+    split_here = dirs_here // box_count
+    rows_here = split_here // PP
+
+    up_phi, up_theta, down_theta, down_phi = tables(channels)
+    cos_table, sin_table = (jnp.asarray(t) for t in np_phase(channels))
+    slots = lax.dynamic_slice_in_dim(fine_slot, dir_index * fine_here, fine_here, 0)
+    alive = jnp.arange(length, dtype=jnp.int32)[None, :] < list_count[:, None]
+    partner = jnp.where(alive, list_partner, -1)
+    rows = lax.dynamic_slice_in_dim(translator, box_index * split_here, split_here, 2)
+    rows = rows.reshape(kinds, 2 * split_here)
+
+    raised = raise_parents(
+        slots, outgoing, parents_here, (jnp.asarray(up_phi), jnp.asarray(up_theta), cos_table, sin_table)
+    )
+    band = lax.psum_scatter(raised, "dir", scatter_dimension=0, tiled=True)
+    operator = build_operator(partner, list_kind, rows, targets)
+    sources = lax.all_to_all(band, "box", split_axis=0, concat_axis=1, tiled=True)
+    incoming = apply_operator(operator, sources, targets)
+    returned = lax.all_to_all(incoming, "box", split_axis=1, concat_axis=0, tiled=True)
+    field = lax.all_gather(returned, "dir", axis=0, tiled=True)
+    return lower_parents(
+        slots, field, (jnp.asarray(down_phi), jnp.asarray(down_theta), cos_table, sin_table)
+    )
+
+
 def solution(mesh):
     placed = (P(("box", "dir"), None, None), P("box"), P(None, None, "dir"), P(), P(), P())
     return jax.shard_map(

time: 439 us -> 181 us (0.41); the launches traced: 434 us -> 180 us
  matrix products: 108 us -> 0 us
  blocking collectives: 108 us -> 14 us
  other arithmetic: 53.1 us -> 0.08 us
  Pallas kernels: 0 us -> 52.2 us
  local copies, waits for them, and re-layouts: 55.8 us -> 8.14 us
  between operations: 0.66 us -> 13.5 us
  waiting for transfers between devices: 96.9 us -> 88.7 us
  starting transfers between devices: 10.9 us -> 3.68 us
    dot_general x20 -> x0, matrix products: 108 us -> none  [the longest x7 48.6 us: add_block(): jnp.dot(select_source, flat_sources, precision=highest, preferred_element...]
    all_to_all x2 -> x1, waiting for transfers between devices: 96.9 us -> 0.01 us  [body(): lax.all_to_all(band, 'box', split_axis=0, concat_axis=1, tiled=True)]
    all_to_all x2 -> x1, blocking collectives: 108 us -> 14 us  [body(): lax.all_to_all(incoming, 'box', split_axis=1, concat_axis=0, tiled=True)]
    pallas_call x0 -> x4, Pallas kernels: none -> 52.2 us  [the longest x1 24.4 us: build_operator(): pl.pallas_call(functools.partial(operator_kernel, targets=targets, source...]
    reduce_scatter x0 -> x1, waiting for transfers between devices: none -> 45.1 us  [body(): band = lax.psum_scatter(raised, 'dir', scatter_dimension=0, tiled=True)]
    all_gather x0 -> x1, waiting for transfers between devices: none -> 43.6 us  [body(): field = lax.all_gather(returned, 'dir', axis=0, tiled=True)]
    reduce_sum x9 -> x0, other arithmetic: 28.8 us -> none  [the longest x7 25.3 us: add_block(): new_real = jnp.sum(along_real * real_part - along_imag * imag_part, axis=1)]
    dot_general x7 -> x0, local copies, waits for them, and re-layouts: 15.3 us -> none  [add_block(): jnp.dot(select_source, flat_sources, precision=highest, preferred_element...]
  transfers between devices with their start and end apart: 2 -> 3, of which waited for: 2 -> 2; matrix products, arithmetic and copies ran while one was open for 1% -> 1% of each run, Pallas kernels for 0% -> 14%
where the time goes in v1:
time: 181 us; the launch traced here: 180 us
  waiting for transfers between devices  88.7 us (49%)
  Pallas kernels  52.2 us (29%)
  blocking collectives  14 us (8%)
  between operations  13.5 us (7%)
  local copies, waits for them, and re-layouts  8.14 us (4%)
  starting transfers between devices  3.68 us (2%)
    reduce_scatter x1, waiting for transfers between devices, body(): band = lax.psum_scatter(raised, 'dir', scatter_dimension=0, tiled=True)  45.1 us
    all_gather x1, waiting for transfers between devices, body(): field = lax.all_gather(returned, 'dir', axis=0, tiled=True)  43.6 us
    pallas_call x1, Pallas kernels, build_operator(): pl.pallas_call(functools.partial(operator_kernel, targets=targets, source...  24.4 us
    all_to_all x1, blocking collectives, body(): lax.all_to_all(incoming, 'box', split_axis=1, concat_axis=0, tiled=True)  14 us
    pallas_call x1, Pallas kernels, raise_parents(): pl.pallas_call(raise_kernel, out_shape=jax.ShapeDtypeStruct(shape, jnp.fl...  9.64 us
    pallas_call x1, Pallas kernels, lower_parents(): pl.pallas_call(lower_kernel, out_shape=jax.ShapeDtypeStruct((fine, channe...  9.53 us
    pallas_call x1, Pallas kernels, apply_operator(): pl.pallas_call(functools.partial(apply_kernel, count=count, targets=targe...  8.57 us
    unnamed x22, local copies, waits for them, and re-layouts  5.18 us
  transfers between devices with their start and end apart: 3, of which 2 were waited for; matrix products, arithmetic and copies ran while one was open for 1% of the time, Pallas kernels for 14%

profile of v1, /device:TPU:0, one launch (start us, length us, event | category | flops | bytes accessed | tf_op | source)
XLA Modules:
  0.0 180.3 jit_solution(12920913693870085506)
XLA Ops:
  6.5 0.7 dynamic_slice.6.slot_ref
  7.3 1.2 copy-done.2
  8.5 1.1 copy-done.4
  9.6 0.9 copy-done.6
  10.6 9.6 %raise_parents.1 = f32[64,8,8,128]{3,2,1,0:T(8,128)} custom-call(s32[16]{0:T(128)S(1)} %dynamic_slice.6.slot_ref, f32[16,8,2048]{2,1,0:T(8,128)S(1)} %copy-done.2, bf16[384,256]{1,0:T(8,128)(2,1)S(1)} %copy-done.6, bf16[512,768]{1,0:T(8,128)(2,1)S(1)} %copy-done.4, f32[8,64,8,128]{3,2,1,0:T(8,128)} %constant.33.clone.cos_ref, ...), custom_call_target="tpu_custom_call" | custom-call | tf_op jit(solution)/shard_map/raise_parents/pallas_call | solution.py:309
  20.2 0.0 reduce-scatter.2.cloned.1.call-update
  20.2 1.3 constant_dynamic-slice_fusion
  21.5 0.0 copy-start.8
  21.6 0.2 pad
  21.9 45.1 %reduce-scatter.2.cloned.1.call-done = f32[16,8,8,128]{3,2,1,0:T(8,128)} async-done(((f32[64,8,8,128]{3,2,1,0:T(8,128)}), f32[16,8,8,128]{3,2,1,0:T(8,128)}) %reduce-scatter.2.cloned.1.call-update) | async-done | bytes 524304 | tf_op jit(solution)/shard_map/reduce_scatter | solution.py:497
  66.9 3.6 %all-to-all-start = ((f32[16,8,8,128]{3,2,1,0:T(8,128)}), f32[16,8,8,128]{3,2,1,0:T(8,128)S(1)}, u32[]{:S(2)}, u32[]{:S(2)}) async-start(f32[16,8,8,128]{3,2,1,0:T(8,128)} %reduce-scatter.2.cloned.1.call-done), calls=%async_computation.1 | async-start | bytes 1048576 | tf_op jit(solution)/shard_map/all_to_all | solution.py:499
  70.6 0.0 all-gather.2.cloned.1.call-start
  70.6 0.1 fusion.partner_ref
  70.7 24.4 %build_operator.1.op_ref = f32[4096,512]{1,0:T(8,128)} custom-call(s32[64,189]{1,0:T(8,128)S(1)} %fusion.partner_ref, s32[64,189]{1,0:T(8,128)S(1)} %copy-done.7, f32[316,512]{1,0:T(8,128)S(1)} %bitcast.14), custom_call_target="tpu_custom_call" | custom-call | flops 3221225472 | bytes 8388608 | tf_op jit(solution)/shard_map/build_operator/pallas_call | solution.py:404
  95.2 8.6 %apply_operator.1 = f32[1024,128]{1,0:T(8,128)S(1)} custom-call(f32[4096,512]{1,0:T(8,128)} %build_operator.1.op_ref, f32[2,64,8,128]{3,2,1,0:T(8,128)S(1)} %bitcast.12), custom_call_target="tpu_custom_call" | custom-call | tf_op jit(solution)/shard_map/apply_operator/pallas_call | solution.py:459
  103.8 0.0 copy-start
  103.8 0.0 copy-start.3
  103.8 0.0 copy-start.5
  103.8 14.0 %all_to_all.36 = f32[2,64,8,128]{3,2,0,1:T(8,128)S(1)} all-to-all(f32[2,64,8,128]{3,2,0,1:T(8,128)S(1)} %copy.20), channel_id=1, replica_groups=mesh['box'=8,'dir'=4] {'box'}, dimensions={1} | all-to-all | bytes 1048576 | tf_op jit(solution)/shard_map/all_to_all | solution.py:501
  117.8 0.9 copy.22
  118.7 0.0 all-gather.2.cloned.1.call-update
  118.7 43.6 %all-gather.2.cloned.1.call-done.f_ref = f32[64,8,8,128]{3,2,1,0:T(8,128)} async-done(((f32[16,8,8,128]{3,2,1,0:T(8,128)}), f32[64,8,8,128]{3,2,1,0:T(8,128)}) %all-gather.2.cloned.1.call-update) | async-done | bytes 2097168 | tf_op jit(solution)/shard_map/all_gather | solution.py:502
  162.3 1.6 copy-done.1
  163.9 9.5 %lower_parents.1 = f32[16,8,2048]{2,1,0:T(8,128)} custom-call(s32[16]{0:T(128)S(1)} %dynamic_slice.6.slot_ref, f32[64,8,8,128]{3,2,1,0:T(8,128)S(1)} %copy-done.1, bf16[768,128]{1,0:T(8,128)(2,1)S(1)} %copy-done.5, bf16[256,1536]{1,0:T(8,128)(2,1)S(1)} %copy-done.3, f32[8,64,8,128]{3,2,1,0:T(8,128)S(1)} %copy-done, f32[8,64,8,128]{3,2,1,0:T(8,128)} %constant.34.clone.sin_ref), custom_call_target="tpu_custom_call" | custom-call | tf_op jit(solution)/shard_map/lower_parents/pallas_call | solution.py:333
  (17 shorter events, 0.1 us)
Async XLA Ops:
  6.5 60.4 %reduce-scatter.2.cloned.1.call-start = ((), (), s32[]{:S(2)}) async-start(), calls=%async_computation.3 | async-start | bytes 2621440 | tf_op jit(solution)/shard_map/reduce_scatter | solution.py:497
  7.3 1.2 copy-start.2
  8.5 1.1 copy-start.4
  9.6 0.9 copy-start.6
  21.5 49.1 %copy-start.8 = (s32[64,189]{1,0:T(8,128)S(1)}, s32[64,189]{1,0:T(8,128)}, u32[]{:S(2)}) copy-start(s32[64,189]{1,0:T(8,128)} %param.15) | copy-start | bytes 145156
  21.5 49.1 %copy-start.9 = (s32[64]{0:T(128)S(1)}, s32[64]{0:T(128)}, u32[]{:S(2)}) copy-start(s32[64]{0:T(128)} %param.17) | copy-start | bytes 772
  21.6 49.2 %copy-start.7 = (s32[64,189]{1,0:T(8,128)S(1)}, s32[64,189]{1,0:T(8,128)}, u32[]{:S(2)}) copy-start(s32[64,189]{1,0:T(8,128)} %kind_ref.1) | copy-start | bytes 145156
  66.9 28.2 %all-to-all-start = ((f32[16,8,8,128]{3,2,1,0:T(8,128)}), f32[16,8,8,128]{3,2,1,0:T(8,128)S(1)}, u32[]{:S(2)}, u32[]{:S(2)}) async-start(f32[16,8,8,128]{3,2,1,0:T(8,128)} %reduce-scatter.2.cloned.1.call-done), calls=%async_computation.1 | async-start | bytes 1048576 | tf_op jit(solution)/shard_map/all_to_all | solution.py:499
  70.6 91.7 %all-gather.2.cloned.1.call-start = ((), (), s32[]{:S(2)}) async-start(), calls=%async_computation.4 | async-start | bytes 2621440 | tf_op jit(solution)/shard_map/all_gather | solution.py:502
  103.8 58.5 %copy-start = (f32[8,64,8,128]{3,2,1,0:T(8,128)S(1)}, f32[8,64,8,128]{3,2,1,0:T(8,128)}, u32[]{:S(2)}) copy-start(f32[8,64,8,128]{3,2,1,0:T(8,128)} %constant.33.clone.cos_ref) | copy-start | bytes 6291460
  103.8 58.5 %copy-start.3 = (bf16[256,1536]{1,0:T(8,128)(2,1)S(1)}, bf16[256,1536]{1,0:T(8,128)(2,1)}, u32[]{:S(2)}) copy-start(bf16[256,1536]{1,0:T(8,128)(2,1)} %constant.38.clone.theta_ref) | copy-start | bytes 2359300
  103.8 58.5 %copy-start.5 = (bf16[768,128]{1,0:T(8,128)(2,1)S(1)}, bf16[768,128]{1,0:T(8,128)(2,1)}, u32[]{:S(2)}) copy-start(bf16[768,128]{1,0:T(8,128)(2,1)} %constant.37.clone.phi_ref) | copy-start | bytes 589828
  162.3 1.6 copy-start.1
Sparse Core Ops, SparseCore 0:
  20.3 46.5 reduce-scatter.1
  118.8 43.4 all-gather.1

commit v2 on v1

--- a/solution.py
+++ b/solution.py
@@ -350,9 +350,158 @@
     )(slots, field, phi, theta, cos_table, sin_table)
 
 
-def fill_operator(partner_ref, kind_ref, rows_ref, sel_ref, store, targets, sources):
+MESH = pl.DeviceIdType.MESH
+
+
+def exchange_kernel(
+    p_ref, partner_ref, kind_ref, rows_ref, out_ref,
+    sel_ref, op_ref, up_ref, down_ref, band_ref, src_ref, res_ref,
+    up_send, up_recv, down_send, down_recv, go_send, go_recv, back_send, back_recv,
+    rise_send, rise_recv, sink_send, sink_recv,
+    *, targets, channels,
+):
+    n, boxes, halves, block, width = p_ref.shape
+    box = lax.axis_index("box")
+    z = lax.axis_index("dir")
+    sources = targets
     blocks = sel_ref.shape[0]
     length = partner_ref.shape[1]
+    pair_rows = sources * targets
+
+    def remote(src, dst, send, recv, to_box, to_dir):
+        return pltpu.make_async_remote_copy(
+            src_ref=src, dst_ref=dst, send_sem=send, recv_sem=recv,
+            device_id=(to_box, to_dir), device_id_type=MESH,
+        )
+
+    def up_copy(h, b, src):
+        return remote(src, up_ref.at[h, b], up_send.at[h, b], up_recv.at[h, b], box, z + 1)
+
+    def down_copy(h, b, src):
+        return remote(src, down_ref.at[h, b], down_send.at[h, b], down_recv.at[h, b], box, z - 1)
+
+    def sum_start(h):
+        @pl.when(z == 0)
+        def _():
+            for b in range(n - 1, 0, -1):
+                up_copy(h, b, p_ref.at[b, :, h]).start()
+
+        @pl.when(z == n - 1)
+        def _():
+            for b in range(n - 1):
+                down_copy(h, b, p_ref.at[b, :, h]).start()
+
+    def sum_step(h, step):
+        up_b = n - 1 - step
+        down_b = step
+
+        @pl.when((z > 0) & (z < up_b))
+        def _():
+            copy = up_copy(h, up_b, up_ref.at[h, up_b])
+            copy.wait_recv()
+            up_ref[h, up_b] += p_ref[up_b, :, h]
+            copy.start()
+
+        @pl.when((z < n - 1) & (z > down_b))
+        def _():
+            copy = down_copy(h, down_b, down_ref.at[h, down_b])
+            copy.wait_recv()
+            down_ref[h, down_b] += p_ref[down_b, :, h]
+            copy.start()
+
+    def sum_finish(h):
+        band_ref[h] = p_ref[z, :, h]
+
+        @pl.when(z > 0)
+        def _():
+            up_copy(h, z, up_ref.at[h, z]).wait_recv()
+            band_ref[h] += up_ref[h, z]
+
+        @pl.when(z < n - 1)
+        def _():
+            down_copy(h, z, down_ref.at[h, z]).wait_recv()
+            band_ref[h] += down_ref[h, z]
+
+    def sum_drain(h):
+        for b in range(n):
+            @pl.when(z < b)
+            def _():
+                up_copy(h, b, up_ref.at[h, b]).wait_send()
+
+            @pl.when(z > b)
+            def _():
+                down_copy(h, b, down_ref.at[h, b]).wait_send()
+
+    def peer(k):
+        return lax.rem(box + k, boxes)
+
+    def go_copy(h, k):
+        return remote(
+            band_ref.at[h, peer(k)], src_ref.at[h, box], go_send.at[h, k], go_recv.at[h, k], peer(k), z
+        )
+
+    def back_copy(h, k):
+        return remote(
+            res_ref.at[h, pl.ds(pl.multiple_of(peer(k) * block, block), block)],
+            out_ref.at[z, box, h],
+            back_send.at[h, k], back_recv.at[h, k], peer(k), z,
+        )
+
+    def go_start(h):
+        for k in range(1, boxes):
+            go_copy(h, k).start()
+        src_ref[h, box] = band_ref[h, box]
+
+    def go_wait(h):
+        for k in range(1, boxes):
+            go_copy(h, k).wait_recv()
+
+    def back_start(h):
+        for k in range(1, boxes):
+            back_copy(h, k).start()
+        out_ref[z, box, h] = res_ref[h, pl.ds(pl.multiple_of(box * block, block), block)]
+
+    def back_wait(h):
+        for k in range(1, boxes):
+            back_copy(h, k).wait_recv()
+
+    def rise_copy(h, b):
+        piece = out_ref.at[b, :, h]
+        return remote(piece, piece, rise_send.at[h, b], rise_recv.at[h, b], box, z + 1)
+
+    def sink_copy(h, b):
+        piece = out_ref.at[b, :, h]
+        return remote(piece, piece, sink_send.at[h, b], sink_recv.at[h, b], box, z - 1)
+
+    def share_step(h, step):
+        @pl.when(z >= step)
+        def _():
+            if step:
+                rise_copy(h, z - step).wait_recv()
+
+            @pl.when(z < n - 1)
+            def _():
+                rise_copy(h, z - step).start()
+
+        @pl.when(z + step <= n - 1)
+        def _():
+            if step:
+                sink_copy(h, z + step).wait_recv()
+
+            @pl.when(z > 0)
+            def _():
+                sink_copy(h, z + step).start()
+
+    def share_drain(h):
+        for b in range(n):
+            @pl.when((z >= b) & (z < n - 1))
+            def _():
+                rise_copy(h, b).wait_send()
+
+            @pl.when((z <= b) & (z > 0))
+            def _():
+                sink_copy(h, b).wait_send()
+
     source_ids = lax.broadcasted_iota(jnp.int32, (sources, length), 0)
     kind_ids = lax.broadcasted_iota(jnp.int32, (blocks * 128, length), 0)
 
@@ -368,103 +517,144 @@
             sel_ref[j, pl.ds(p, sources, stride=targets), :] = counts[:, j * 128 : (j + 1) * 128]
         return 0
 
-    lax.fori_loop(0, targets, count_pairs, 0)
-    kinds, width = rows_ref.shape
-    pad = blocks * 128 - kinds
-    rows = rows_ref[...]
-    if pad:
-        rows = jnp.concatenate([rows, jnp.zeros((pad, width), jnp.float32)], axis=0)
-    high = rows.astype(jnp.bfloat16)
-    low = (rows - high.astype(jnp.float32)).astype(jnp.bfloat16)
-    both = jnp.concatenate([high, low], axis=0)
-    tile = 512
-
-    def one_tile(i, _):
-        start = pl.multiple_of(i * tile, tile)
-        chosen = jnp.concatenate(
-            [sel_ref[j, pl.ds(start, tile), :] for j in range(blocks)], axis=1
-        ).astype(jnp.bfloat16)
-        store(start, tile, dot(jnp.concatenate([chosen, chosen], axis=1), both))
-        return 0
-
-    lax.fori_loop(0, targets * sources // tile, one_tile, 0)
-
-
-def operator_kernel(partner_ref, kind_ref, rows_ref, out_ref, sel_ref, *, targets, sources):
-    def store(start, tile, values):
-        out_ref[pl.ds(start, tile), :] = values
-
-    fill_operator(partner_ref, kind_ref, rows_ref, sel_ref, store, targets, sources)
-
-
-def build_operator(partner, kind, rows, sources):
-    targets, length = partner.shape
-    kinds, width = rows.shape
-    blocks = -(-kinds // 128)
-    return pl.pallas_call(
-        functools.partial(operator_kernel, targets=targets, sources=sources),
-        out_shape=jax.ShapeDtypeStruct((sources * targets, width), jnp.float32),
-        scratch_shapes=[pltpu.VMEM((blocks, sources * targets, 128), jnp.float32)],
-        compiler_params=pltpu.CompilerParams(vmem_limit_bytes=48 * 2**20),
-        cost_estimate=pl.CostEstimate(
-            flops=4 * sources * targets * blocks * 128 * width,
-            bytes_accessed=4 * sources * targets * width,
-            transcendentals=0,
+    def count_part(part, parts):
+        first, last = targets * part // parts, targets * (part + 1) // parts
+        lax.fori_loop(first, last, count_pairs, 0, unroll=4)
+
+    def operator_half(h):
+        rows = jnp.concatenate(
+            [rows_ref[:, i * width : (i + 1) * width] for i in (h, halves + h)], axis=1
+        )
+        pad = blocks * 128 - rows.shape[0]
+        if pad:
+            rows = jnp.concatenate([rows, jnp.zeros((pad, 2 * width), jnp.float32)], axis=0)
+        high = rows.astype(jnp.bfloat16)
+        low = (rows - high.astype(jnp.float32)).astype(jnp.bfloat16)
+        both = jnp.concatenate([high, low], axis=0)
+        tile = 512
+
+        def one_tile(i, _):
+            start = pl.multiple_of(i * tile, tile)
+            chosen = jnp.concatenate(
+                [sel_ref[j, pl.ds(start, tile), :] for j in range(blocks)], axis=1
+            ).astype(jnp.bfloat16)
+            op_ref[h, pl.ds(start, tile), :] = dot(
+                jnp.concatenate([chosen, chosen], axis=1), both
+            )
+            return 0
+
+        lax.fori_loop(0, pair_rows // tile, one_tile, 0)
+
+    def apply_half(h):
+        half = channels // 2
+        group = 2
+        per_box = block // channels
+
+        def add_source(s, sums, first):
+            giver = s // per_box
+            row0 = (s % per_box) * channels
+            fields = [src_ref[h, giver, pl.ds(row0 + c, 1), :] for c in range(channels)]
+            out = []
+            for g in range(group):
+                row = pl.multiple_of(s * targets + first + g * 8, 8)
+                real = op_ref[h, pl.ds(row, 8), 0:width]
+                imag = op_ref[h, pl.ds(row, 8), width : 2 * width]
+                mine = sums[g * channels : (g + 1) * channels]
+                for e in range(half):
+                    out.append(mine[e] + real * fields[e] - imag * fields[half + e])
+                for e in range(half):
+                    out.append(mine[half + e] + real * fields[half + e] + imag * fields[e])
+            return tuple(out)
+
+        for first in range(0, targets, group * 8):
+            sums = tuple(jnp.zeros((8, width), jnp.float32) for _ in range(group * channels))
+            sums = lax.fori_loop(
+                0, sources, functools.partial(add_source, first=first), sums, unroll=4
+            )
+            for g in range(group):
+                for c in range(channels):
+                    start = (first + g * 8) * channels + c
+                    res_ref[h, pl.ds(start, 8, stride=channels), :] = sums[g * channels + c]
+
+    barrier = pltpu.get_barrier_semaphore()
+    for k in range(1, boxes):
+        pl.semaphore_signal(barrier, inc=1, device_id=(peer(k), z), device_id_type=MESH)
+
+    @pl.when(z > 0)
+    def _():
+        pl.semaphore_signal(barrier, inc=1, device_id=(box, z - 1), device_id_type=MESH)
+
+    @pl.when(z < n - 1)
+    def _():
+        pl.semaphore_signal(barrier, inc=1, device_id=(box, z + 1), device_id_type=MESH)
+
+    ends = jnp.where(z > 0, 1, 0) + jnp.where(z < n - 1, 1, 0)
+    pl.semaphore_wait(barrier, boxes - 1 + ends)
+
+    for h in range(halves):
+        sum_start(h)
+    for h in range(halves):
+        for step in range(n - 1):
+            if h == 0:
+                count_part(step, n - 1)
+            sum_step(h, step)
+        sum_finish(h)
+        go_start(h)
+        operator_half(h)
+        if h:
+            back_wait(h - 1)
+            share_step(h - 1, 0)
+        go_wait(h)
+        apply_half(h)
+        back_start(h)
+        if h:
+            share_step(h - 1, 1)
+    last = halves - 1
+    back_wait(last)
+    share_step(last, 0)
+    for h in range(halves):
+        for step in range(2 if h < last else 1, n):
+            share_step(h, step)
+    for h in range(halves):
+        sum_drain(h)
+        share_drain(h)
+        for k in range(1, boxes):
+            go_copy(h, k).wait_send()
+            back_copy(h, k).wait_send()
+
+
+def exchange(raised, partner, kind, rows, n, boxes, targets):
+    polar, parents, channels, width = raised.shape
+    halves = polar // n // boxes
+    block = parents * channels
+    kinds = rows.shape[0]
+    kind_blocks = -(-kinds // 128)
+    shape = (n, boxes, halves, block, width)
+    vmem = pl.BlockSpec(memory_space=pltpu.VMEM)
+    dma = pltpu.SemaphoreType.DMA
+    out = pl.pallas_call(
+        functools.partial(exchange_kernel, targets=targets, channels=channels),
+        out_shape=jax.ShapeDtypeStruct(shape, jnp.float32),
+        in_specs=[vmem] * 4,
+        out_specs=vmem,
+        scratch_shapes=[
+            pltpu.VMEM((kind_blocks, targets * targets, 128), jnp.float32),
+            pltpu.VMEM((halves, targets * targets, 2 * width), jnp.float32),
+            pltpu.VMEM((halves, n, boxes, block, width), jnp.float32),
+            pltpu.VMEM((halves, n, boxes, block, width), jnp.float32),
+            pltpu.VMEM((halves, boxes, block, width), jnp.float32),
+            pltpu.VMEM((halves, boxes, block, width), jnp.float32),
+            pltpu.VMEM((halves, targets * channels, width), jnp.float32),
+        ]
+        + [dma((halves, n))] * 4
+        + [dma((halves, boxes))] * 4
+        + [dma((halves, n))] * 4,
+        compiler_params=pltpu.CompilerParams(
+            vmem_limit_bytes=52 * 2**20, collective_id=0, has_side_effects=True
         ),
-        name="build_operator",
-    )(partner, kind, rows)
-
-
-def apply_tiles(op_ref, load, store, u, count, targets, sources, channels):
-    half = channels // 2
-    group = 2
-
-    def add_source(s, sums, first):
-        fields = [load(u, s, c) for c in range(channels)]
-        out = []
-        for g in range(group):
-            row = pl.multiple_of(s * targets + first + g * 8, 8)
-            real = op_ref[pl.ds(row, 8), u * PP : (u + 1) * PP]
-            imag = op_ref[pl.ds(row, 8), (count + u) * PP : (count + u + 1) * PP]
-            mine = sums[g * channels : (g + 1) * channels]
-            for e in range(half):
-                out.append(mine[e] + real * fields[e] - imag * fields[half + e])
-            for e in range(half):
-                out.append(mine[half + e] + real * fields[half + e] + imag * fields[e])
-        return tuple(out)
-
-    for first in range(0, targets, group * 8):
-        sums = tuple(jnp.zeros((8, PP), jnp.float32) for _ in range(group * channels))
-        sums = lax.fori_loop(
-            0, sources, functools.partial(add_source, first=first), sums, unroll=4
-        )
-        for g in range(group):
-            for c in range(channels):
-                store(u, first + g * 8, c, sums[g * channels + c])
-
-
-def apply_kernel(op_ref, s_ref, out_ref, *, count, targets, sources, channels):
-    def load(u, s, c):
-        return s_ref[u, pl.ds(s, 1), c, :]
-
-    def store(u, p, c, values):
-        out_ref[pl.ds((u * targets + p) * channels + c, 8, stride=channels), :] = values
-
-    for u in range(count):
-        apply_tiles(op_ref, load, store, u, count, targets, sources, channels)
-
-
-def apply_operator(operator, fields, targets):
-    count, sources, channels, _ = fields.shape
-    out = pl.pallas_call(
-        functools.partial(
-            apply_kernel, count=count, targets=targets, sources=sources, channels=channels
-        ),
-        out_shape=jax.ShapeDtypeStruct((count * targets * channels, PP), jnp.float32),
-        compiler_params=pltpu.CompilerParams(vmem_limit_bytes=48 * 2**20),
-        name="apply_operator",
-    )(operator, fields)
-    return out.reshape(count, targets, channels, PP)
+        name="exchange",
+    )(raised.reshape(shape), partner, kind, rows)
+    return out.reshape(raised.shape)
 
 
 def body(outgoing, fine_slot, translator, list_partner, list_kind, list_count):
@@ -494,12 +684,7 @@
     raised = raise_parents(
         slots, outgoing, parents_here, (jnp.asarray(up_phi), jnp.asarray(up_theta), cos_table, sin_table)
     )
-    band = lax.psum_scatter(raised, "dir", scatter_dimension=0, tiled=True)
-    operator = build_operator(partner, list_kind, rows, targets)
-    sources = lax.all_to_all(band, "box", split_axis=0, concat_axis=1, tiled=True)
-    incoming = apply_operator(operator, sources, targets)
-    returned = lax.all_to_all(incoming, "box", split_axis=1, concat_axis=0, tiled=True)
-    field = lax.all_gather(returned, "dir", axis=0, tiled=True)
+    field = exchange(raised, partner, list_kind, rows, dir_count, box_count, targets)
     return lower_parents(
         slots, field, (jnp.asarray(down_phi), jnp.asarray(down_theta), cos_table, sin_table)
     )

time: 181 us -> 128 us (0.71)
  waiting for transfers between devices: 88.7 us -> 0 us
  Pallas kernels: 52.2 us -> 121 us
  blocking collectives: 14 us -> 0 us
  between operations: 13.5 us -> 0.12 us
  starting transfers between devices: 3.68 us -> 0 us
  local copies, waits for them, and re-layouts: 8.14 us -> 5.41 us
    pallas_call x2 -> x1, Pallas kernels: 33 us -> 104 us  [exchange(): pl.pallas_call(functools.partial(exchange_kernel, targets=targets, channe...]
    reduce_scatter x1 -> x0, waiting for transfers between devices: 45.1 us -> none  [body(): band = lax.psum_scatter(raised, 'dir', scatter_dimension=0, tiled=True)]
    all_gather x1 -> x0, waiting for transfers between devices: 43.6 us -> none  [body(): field = lax.all_gather(returned, 'dir', axis=0, tiled=True)]
    all_to_all x1 -> x0, blocking collectives: 14 us -> none  [body(): lax.all_to_all(incoming, 'box', split_axis=1, concat_axis=0, tiled=True)]
    all_to_all x1 -> x0, starting transfers between devices: 3.64 us -> none  [body(): lax.all_to_all(band, 'box', split_axis=0, concat_axis=1, tiled=True)]
    unnamed x22 -> x20, local copies, waits for them, and re-layouts: 5.18 us -> 3.22 us
  transfers between devices with their start and end apart: 3 -> 0, of which waited for: 2 -> 0; matrix products, arithmetic and copies ran while one was open for 1% -> 0% of each run, Pallas kernels for 14% -> 0%
where the time goes in v2:
time: 128 us
  Pallas kernels  121 us (95%)
  local copies, waits for them, and re-layouts  5.41 us (4%)
    pallas_call x1, Pallas kernels, exchange(): pl.pallas_call(functools.partial(exchange_kernel, targets=targets, channe...  104 us
    pallas_call x1, Pallas kernels, lower_parents(): pl.pallas_call(lower_kernel, out_shape=jax.ShapeDtypeStruct((fine, channe...  9.63 us
    pallas_call x1, Pallas kernels, raise_parents(): pl.pallas_call(raise_kernel, out_shape=jax.ShapeDtypeStruct(shape, jnp.fl...  8.29 us
    unnamed x20, local copies, waits for them, and re-layouts  3.22 us

profile of v2, /device:TPU:0, one launch (start us, length us, event | category | flops | bytes accessed | tf_op | source)
XLA Modules:
  0.0 127.9 jit_solution(5463059463301008524)
XLA Ops:
  0.0 0.0 copy-start.5
  0.0 0.0 copy-start.7
  0.0 0.0 copy-start.3
  0.0 0.9 dynamic_slice.6.slot_ref
  0.9 0.9 fusion.partner_ref
  1.8 1.3 %constant_dynamic-slice_fusion = f32[316,2,256]{2,1,0:T(2,128)S(1)} fusion(f32[316,2,2048]{2,1,0:T(2,128)} %param.14, s32[]{:T(128)S(6)} %select_n.12), kind=kLoop, calls=%fused_computation.2 | loop fusion | bytes 1294340 | tf_op jit(solution)/shard_map/dynamic_slice | solution.py:681
  3.1 0.2 pad
  3.4 0.0 copy-done.5
  3.4 0.0 copy-done.7
  3.4 0.0 copy-done.3
  3.4 0.0 copy-start.8
  3.4 8.3 %raise_parents.1 = f32[64,8,8,128]{3,2,1,0:T(8,128)S(1)} custom-call(s32[16]{0:T(128)S(1)} %dynamic_slice.6.slot_ref, f32[16,8,2048]{2,1,0:T(8,128)S(1)} %copy-done.3, bf16[384,256]{1,0:T(8,128)(2,1)S(1)} %copy-done.7, bf16[512,768]{1,0:T(8,128)(2,1)S(1)} %copy-done.5, f32[8,64,8,128]{3,2,1,0:T(8,128)} %constant.33.clone.cos_ref, ...), custom_call_target="tpu_custom_call" | custom-call | tf_op jit(solution)/shard_map/raise_parents/pallas_call | solution.py:309
  11.7 0.0 copy-start.1
  11.8 1.3 %copy-done.1 = f32[64,8,8,128]{3,2,1,0:T(8,128)} copy-done((f32[64,8,8,128]{3,2,1,0:T(8,128)}, f32[64,8,8,128]{3,2,1,0:T(8,128)S(1)}, u32[]{:S(2)}) %copy-start.1) | copy-done | bytes 2097176
  13.1 0.0 copy-done.8
  13.1 0.0 copy-start.2
  13.1 0.0 copy-start.4
  13.1 103.5 %exchange.1 = f32[4,8,2,64,128]{4,3,2,1,0:T(8,128)} custom-call(f32[4,8,2,64,128]{4,3,2,1,0:T(8,128)} %bitcast.6, s32[64,189]{1,0:T(8,128)S(1)} %fusion.partner_ref, s32[64,189]{1,0:T(8,128)S(1)} %copy-done.8, f32[316,512]{1,0:T(8,128)S(1)} %bitcast.7), custom_call_target="tpu_custom_call" | custom-call | tf_op jit(solution)/shard_map/exchange/pallas_call | solution.py:635
  116.6 0.0 copy-done.2
  116.7 0.0 copy-done.4
  116.7 0.0 copy-done.6
  116.7 0.0 copy-start
  116.7 1.6 %copy-done = f32[4,8,2,64,128]{4,3,2,1,0:T(8,128)S(1)} copy-done((f32[4,8,2,64,128]{4,3,2,1,0:T(8,128)S(1)}, f32[4,8,2,64,128]{4,3,2,1,0:T(8,128)}, u32[]{:S(2)}) %copy-start) | copy-done | bytes 2097176
  118.3 9.6 %lower_parents.1 = f32[16,8,2048]{2,1,0:T(8,128)} custom-call(s32[16]{0:T(128)S(1)} %dynamic_slice.6.slot_ref, f32[64,8,8,128]{3,2,1,0:T(8,128)S(1)} %bitcast.5, bf16[768,128]{1,0:T(8,128)(2,1)S(1)} %copy-done.6, bf16[256,1536]{1,0:T(8,128)(2,1)S(1)} %copy-done.4, f32[8,64,8,128]{3,2,1,0:T(8,128)S(1)} %copy-done.2, f32[8,64,8,128]{3,2,1,0:T(8,128)} %constant.34.clone.sin_ref), custom_call_target="tpu_custom_call" | custom-call | tf_op jit(solution)/shard_map/lower_parents/pallas_call | solution.py:333
  (2 shorter events, 0.0 us)
Async XLA Ops:
  0.0 3.4 %copy-start.5 = (bf16[512,768]{1,0:T(8,128)(2,1)S(1)}, bf16[512,768]{1,0:T(8,128)(2,1)}, u32[]{:S(2)}) copy-start(bf16[512,768]{1,0:T(8,128)(2,1)} %constant.36.clone.theta_ref) | copy-start | bytes 2359300
  0.0 3.4 %copy-start.7 = (bf16[384,256]{1,0:T(8,128)(2,1)S(1)}, bf16[384,256]{1,0:T(8,128)(2,1)}, u32[]{:S(2)}) copy-start(bf16[384,256]{1,0:T(8,128)(2,1)} %constant.35.clone.phi_ref) | copy-start | bytes 589828
  0.0 3.4 %copy-start.3 = (f32[16,8,2048]{2,1,0:T(8,128)S(1)}, f32[16,8,2048]{2,1,0:T(8,128)}, u32[]{:S(2)}) copy-start(f32[16,8,2048]{2,1,0:T(8,128)} %x_ref.1) | copy-start | bytes 3145732
  3.4 9.7 %copy-start.8 = (s32[64,189]{1,0:T(8,128)S(1)}, s32[64,189]{1,0:T(8,128)}, u32[]{:S(2)}) copy-start(s32[64,189]{1,0:T(8,128)} %kind_ref.1) | copy-start | bytes 145156
  11.7 1.3 %copy-start.1 = (f32[64,8,8,128]{3,2,1,0:T(8,128)}, f32[64,8,8,128]{3,2,1,0:T(8,128)S(1)}, u32[]{:S(2)}) copy-start(f32[64,8,8,128]{3,2,1,0:T(8,128)S(1)} %raise_parents.1) | copy-start | bytes 6291460
  13.1 103.6 %copy-start.2 = (f32[8,64,8,128]{3,2,1,0:T(8,128)S(1)}, f32[8,64,8,128]{3,2,1,0:T(8,128)}, u32[]{:S(2)}) copy-start(f32[8,64,8,128]{3,2,1,0:T(8,128)} %constant.33.clone.cos_ref) | copy-start | bytes 6291460
  13.1 103.6 %copy-start.4 = (bf16[256,1536]{1,0:T(8,128)(2,1)S(1)}, bf16[256,1536]{1,0:T(8,128)(2,1)}, u32[]{:S(2)}) copy-start(bf16[256,1536]{1,0:T(8,128)(2,1)} %constant.38.clone.theta_ref) | copy-start | bytes 2359300
  13.1 103.6 %copy-start.6 = (bf16[768,128]{1,0:T(8,128)(2,1)S(1)}, bf16[768,128]{1,0:T(8,128)(2,1)}, u32[]{:S(2)}) copy-start(bf16[768,128]{1,0:T(8,128)(2,1)} %constant.37.clone.phi_ref) | copy-start | bytes 589828
  116.7 1.6 %copy-start = (f32[4,8,2,64,128]{4,3,2,1,0:T(8,128)S(1)}, f32[4,8,2,64,128]{4,3,2,1,0:T(8,128)}, u32[]{:S(2)}) copy-start(f32[4,8,2,64,128]{4,3,2,1,0:T(8,128)} %exchange.1) | copy-start | bytes 6291460

commit v3 on v2

--- a/solution.py
+++ b/solution.py
@@ -380,35 +380,49 @@
     def down_copy(h, b, src):
         return remote(src, down_ref.at[h, b], down_send.at[h, b], down_recv.at[h, b], box, z - 1)
 
-    def sum_start(h):
+    chunks = n - 1
+
+    def sum_send(g):
+        if g >= halves * chunks:
+            return
+        h, j = divmod(g, chunks)
+
         @pl.when(z == 0)
         def _():
-            for b in range(n - 1, 0, -1):
-                up_copy(h, b, p_ref.at[b, :, h]).start()
+            if g >= 2:
+                h2, j2 = divmod(g - 2, chunks)
+                up_copy(h2, n - 1 - j2, p_ref.at[n - 1 - j2, :, h2]).wait_send()
+            up_copy(h, n - 1 - j, p_ref.at[n - 1 - j, :, h]).start()
 
         @pl.when(z == n - 1)
         def _():
-            for b in range(n - 1):
-                down_copy(h, b, p_ref.at[b, :, h]).start()
-
-    def sum_step(h, step):
-        up_b = n - 1 - step
-        down_b = step
-
-        @pl.when((z > 0) & (z < up_b))
+            if g >= 2:
+                h2, j2 = divmod(g - 2, chunks)
+                down_copy(h2, j2, p_ref.at[j2, :, h2]).wait_send()
+            down_copy(h, j, p_ref.at[j, :, h]).start()
+
+    def sum_tick(tick):
+        h = (tick - 1) // chunks
+        j = tick - h * chunks
+        up_b = n - 1 - j + z
+        down_b = j - (n - 1 - z)
+
+        @pl.when((z > 0) & (z < up_b) & (up_b < n))
         def _():
             copy = up_copy(h, up_b, up_ref.at[h, up_b])
             copy.wait_recv()
             up_ref[h, up_b] += p_ref[up_b, :, h]
             copy.start()
 
-        @pl.when((z < n - 1) & (z > down_b))
+        @pl.when((z < n - 1) & (z > down_b) & (down_b >= 0))
         def _():
             copy = down_copy(h, down_b, down_ref.at[h, down_b])
             copy.wait_recv()
             down_ref[h, down_b] += p_ref[down_b, :, h]
             copy.start()
 
+        sum_send(tick + 1)
+
     def sum_finish(h):
         band_ref[h] = p_ref[z, :, h]
 
@@ -424,13 +438,23 @@
 
     def sum_drain(h):
         for b in range(n):
-            @pl.when(z < b)
+            @pl.when((z < b) & (z > 0))
             def _():
                 up_copy(h, b, up_ref.at[h, b]).wait_send()
 
-            @pl.when(z > b)
+            @pl.when((z > b) & (z < n - 1))
             def _():
                 down_copy(h, b, down_ref.at[h, b]).wait_send()
+
+        for j in range(chunks):
+            if h * chunks + j >= halves * chunks - 2:
+                @pl.when(z == 0)
+                def _():
+                    up_copy(h, n - 1 - j, p_ref.at[n - 1 - j, :, h]).wait_send()
+
+                @pl.when(z == n - 1)
+                def _():
+                    down_copy(h, j, p_ref.at[j, :, h]).wait_send()
 
     def peer(k):
         return lax.rem(box + k, boxes)
@@ -545,7 +569,7 @@
 
         lax.fori_loop(0, pair_rows // tile, one_tile, 0)
 
-    def apply_half(h):
+    def apply_half(h, part, parts):
         half = channels // 2
         group = 2
         per_box = block // channels
@@ -566,7 +590,7 @@
                     out.append(mine[half + e] + real * fields[half + e] + imag * fields[e])
             return tuple(out)
 
-        for first in range(0, targets, group * 8):
+        for first in range(targets * part // parts, targets * (part + 1) // parts, group * 8):
             sums = tuple(jnp.zeros((8, width), jnp.float32) for _ in range(group * channels))
             sums = lax.fori_loop(
                 0, sources, functools.partial(add_source, first=first), sums, unroll=4
@@ -591,29 +615,40 @@
     ends = jnp.where(z > 0, 1, 0) + jnp.where(z < n - 1, 1, 0)
     pl.semaphore_wait(barrier, boxes - 1 + ends)
 
+    sum_send(0)
+    sum_send(1)
     for h in range(halves):
-        sum_start(h)
-    for h in range(halves):
-        for step in range(n - 1):
-            if h == 0:
-                count_part(step, n - 1)
-            sum_step(h, step)
+        tick = h * chunks
+        for step in range(1, chunks + 1):
+            if h == 0 and step < chunks:
+                count_part(step - 1, chunks - 1)
+            if h == 0 and step == chunks:
+                operator_half(h)
+            if h and step == 1:
+                apply_half(h - 1, 0, 2)
+            if h and step == 2:
+                apply_half(h - 1, 1, 2)
+                back_start(h - 1)
+            if h and step == chunks:
+                back_wait(h - 1)
+                share_step(h - 1, 0)
+                operator_half(h)
+            sum_tick(tick + step)
         sum_finish(h)
         go_start(h)
-        operator_half(h)
-        if h:
-            back_wait(h - 1)
-            share_step(h - 1, 0)
-        go_wait(h)
-        apply_half(h)
-        back_start(h)
         if h:
             share_step(h - 1, 1)
+        go_wait(h)
+    apply_half(halves - 1, 0, 2)
+    apply_half(halves - 1, 1, 2)
+    back_start(halves - 1)
+    if halves > 1:
+        share_step(halves - 2, 2)
     last = halves - 1
     back_wait(last)
     share_step(last, 0)
     for h in range(halves):
-        for step in range(2 if h < last else 1, n):
+        for step in range(3 if h == last - 1 else 1, n):
             share_step(h, step)
     for h in range(halves):
         sum_drain(h)

time: 128 us -> 111 us (0.87)
  Pallas kernels: 121 us -> 104 us
    pallas_call x1, Pallas kernels: 104 us -> 86 us  [exchange(): pl.pallas_call(functools.partial(exchange_kernel, targets=targets, channe...]
where the time goes in v3:
time: 111 us; the launch traced here: 110 us
  Pallas kernels  104 us (94%)
  local copies, waits for them, and re-layouts  5.41 us (5%)
    pallas_call x1, Pallas kernels, exchange(): pl.pallas_call(functools.partial(exchange_kernel, targets=targets, channe...  86 us
    pallas_call x1, Pallas kernels, lower_parents(): pl.pallas_call(lower_kernel, out_shape=jax.ShapeDtypeStruct((fine, channe...  9.62 us
    pallas_call x1, Pallas kernels, raise_parents(): pl.pallas_call(raise_kernel, out_shape=jax.ShapeDtypeStruct(shape, jnp.fl...  8.29 us
    unnamed x20, local copies, waits for them, and re-layouts  3.22 us

profile of v3, /device:TPU:0, one launch (start us, length us, event | category | flops | bytes accessed | tf_op | source)
XLA Modules:
  0.0 110.4 jit_solution(14158815205547278907)
XLA Ops:
  0.0 0.0 copy-start.5
  0.0 0.0 copy-start.7
  0.0 0.0 copy-start.3
  0.0 0.9 dynamic_slice.6.slot_ref
  0.9 0.9 fusion.partner_ref
  1.8 1.3 %constant_dynamic-slice_fusion = f32[316,2,256]{2,1,0:T(2,128)S(1)} fusion(f32[316,2,2048]{2,1,0:T(2,128)} %param.14, s32[]{:T(128)S(6)} %select_n.12), kind=kLoop, calls=%fused_computation.2 | loop fusion | bytes 1294340 | tf_op jit(solution)/shard_map/dynamic_slice | solution.py:716
  3.1 0.2 pad
  3.4 0.0 copy-done.5
  3.4 0.0 copy-done.7
  3.4 0.0 copy-done.3
  3.4 0.0 copy-start.8
  3.4 8.3 %raise_parents.1 = f32[64,8,8,128]{3,2,1,0:T(8,128)S(1)} custom-call(s32[16]{0:T(128)S(1)} %dynamic_slice.6.slot_ref, f32[16,8,2048]{2,1,0:T(8,128)S(1)} %copy-done.3, bf16[384,256]{1,0:T(8,128)(2,1)S(1)} %copy-done.7, bf16[512,768]{1,0:T(8,128)(2,1)S(1)} %copy-done.5, f32[8,64,8,128]{3,2,1,0:T(8,128)} %constant.33.clone.cos_ref, ...), custom_call_target="tpu_custom_call" | custom-call | tf_op jit(solution)/shard_map/raise_parents/pallas_call | solution.py:309
  11.7 0.0 copy-start.1
  11.8 1.3 %copy-done.1 = f32[64,8,8,128]{3,2,1,0:T(8,128)} copy-done((f32[64,8,8,128]{3,2,1,0:T(8,128)}, f32[64,8,8,128]{3,2,1,0:T(8,128)S(1)}, u32[]{:S(2)}) %copy-start.1) | copy-done | bytes 2097176
  13.1 0.0 copy-done.8
  13.1 0.0 copy-start.2
  13.1 0.0 copy-start.6
  13.1 86.0 %exchange.1 = f32[4,8,2,64,128]{4,3,2,1,0:T(8,128)} custom-call(f32[4,8,2,64,128]{4,3,2,1,0:T(8,128)} %bitcast.6, s32[64,189]{1,0:T(8,128)S(1)} %fusion.partner_ref, s32[64,189]{1,0:T(8,128)S(1)} %copy-done.8, f32[316,512]{1,0:T(8,128)S(1)} %bitcast.7), custom_call_target="tpu_custom_call" | custom-call | tf_op jit(solution)/shard_map/exchange/pallas_call | solution.py:670
  99.1 0.0 copy-done.2
  99.1 0.0 copy-done.4
  99.1 0.0 copy-done.6
  99.2 0.0 copy-start
  99.2 1.6 %copy-done = f32[4,8,2,64,128]{4,3,2,1,0:T(8,128)S(1)} copy-done((f32[4,8,2,64,128]{4,3,2,1,0:T(8,128)S(1)}, f32[4,8,2,64,128]{4,3,2,1,0:T(8,128)}, u32[]{:S(2)}) %copy-start) | copy-done | bytes 2097176
  100.7 9.6 %lower_parents.1 = f32[16,8,2048]{2,1,0:T(8,128)} custom-call(s32[16]{0:T(128)S(1)} %dynamic_slice.6.slot_ref, f32[64,8,8,128]{3,2,1,0:T(8,128)S(1)} %bitcast.5, bf16[768,128]{1,0:T(8,128)(2,1)S(1)} %copy-done.6, bf16[256,1536]{1,0:T(8,128)(2,1)S(1)} %copy-done.4, f32[8,64,8,128]{3,2,1,0:T(8,128)S(1)} %copy-done.2, f32[8,64,8,128]{3,2,1,0:T(8,128)} %constant.34.clone.sin_ref), custom_call_target="tpu_custom_call" | custom-call | tf_op jit(solution)/shard_map/lower_parents/pallas_call | solution.py:333
  (2 shorter events, 0.0 us)
Async XLA Ops:
  0.0 3.4 %copy-start.5 = (bf16[512,768]{1,0:T(8,128)(2,1)S(1)}, bf16[512,768]{1,0:T(8,128)(2,1)}, u32[]{:S(2)}) copy-start(bf16[512,768]{1,0:T(8,128)(2,1)} %constant.36.clone.theta_ref) | copy-start | bytes 2359300
  0.0 3.4 %copy-start.7 = (bf16[384,256]{1,0:T(8,128)(2,1)S(1)}, bf16[384,256]{1,0:T(8,128)(2,1)}, u32[]{:S(2)}) copy-start(bf16[384,256]{1,0:T(8,128)(2,1)} %constant.35.clone.phi_ref) | copy-start | bytes 589828
  0.0 3.4 %copy-start.3 = (f32[16,8,2048]{2,1,0:T(8,128)S(1)}, f32[16,8,2048]{2,1,0:T(8,128)}, u32[]{:S(2)}) copy-start(f32[16,8,2048]{2,1,0:T(8,128)} %x_ref.1) | copy-start | bytes 3145732
  3.4 9.7 %copy-start.8 = (s32[64,189]{1,0:T(8,128)S(1)}, s32[64,189]{1,0:T(8,128)}, u32[]{:S(2)}) copy-start(s32[64,189]{1,0:T(8,128)} %kind_ref.1) | copy-start | bytes 145156
  11.7 1.3 %copy-start.1 = (f32[64,8,8,128]{3,2,1,0:T(8,128)}, f32[64,8,8,128]{3,2,1,0:T(8,128)S(1)}, u32[]{:S(2)}) copy-start(f32[64,8,8,128]{3,2,1,0:T(8,128)S(1)} %raise_parents.1) | copy-start | bytes 6291460
  13.1 86.0 %copy-start.2 = (f32[8,64,8,128]{3,2,1,0:T(8,128)S(1)}, f32[8,64,8,128]{3,2,1,0:T(8,128)}, u32[]{:S(2)}) copy-start(f32[8,64,8,128]{3,2,1,0:T(8,128)} %constant.33.clone.cos_ref) | copy-start | bytes 6291460
  13.1 86.0 %copy-start.4 = (bf16[256,1536]{1,0:T(8,128)(2,1)S(1)}, bf16[256,1536]{1,0:T(8,128)(2,1)}, u32[]{:S(2)}) copy-start(bf16[256,1536]{1,0:T(8,128)(2,1)} %constant.38.clone.theta_ref) | copy-start | bytes 2359300
  13.1 86.1 %copy-start.6 = (bf16[768,128]{1,0:T(8,128)(2,1)S(1)}, bf16[768,128]{1,0:T(8,128)(2,1)}, u32[]{:S(2)}) copy-start(bf16[768,128]{1,0:T(8,128)(2,1)} %constant.37.clone.phi_ref) | copy-start | bytes 589828
  99.2 1.6 %copy-start = (f32[4,8,2,64,128]{4,3,2,1,0:T(8,128)S(1)}, f32[4,8,2,64,128]{4,3,2,1,0:T(8,128)}, u32[]{:S(2)}) copy-start(f32[4,8,2,64,128]{4,3,2,1,0:T(8,128)} %exchange.1) | copy-start | bytes 6291460

commit v4 on v3

--- a/solution.py
+++ b/solution.py
@@ -187,22 +187,21 @@
     return (1.0 + 2.0 * series + np.cos(offset * (fine_count // 2))) / fine_count
 
 
-def np_phase(channels):
+def np_phase():
     polar = (np.arange(TP) + 0.5) * (np.pi / TP)
     azimuth = np.arange(PP) * (2.0 * np.pi / PP)
-    octant = np.arange(8)
-    signs = [2.0 * (octant // step % 2) - 1.0 for step in (1, 2, 4)]
     along = [
         np.sin(polar)[:, None] * np.cos(azimuth)[None, :],
         np.sin(polar)[:, None] * np.sin(azimuth)[None, :],
         np.cos(polar)[:, None] + 0.0 * azimuth[None, :],
     ]
-    angle = wave_shift * sum(s[:, None, None] * a[None] for s, a in zip(signs, along))
-    half = channels // 2
-    turn = np.where(np.arange(channels) < half, 1.0, -1.0)
-    sin_table = np.sin(angle)[:, :, None, :] * turn[None, None, :, None]
-    cos_table = np.broadcast_to(np.cos(angle)[:, :, None, :], sin_table.shape)
-    return cos_table.astype(np.float32), sin_table.astype(np.float32)
+    cx, cy, cz = (np.cos(wave_shift * a) for a in along)
+    sx, sy, sz = (np.sin(wave_shift * a) for a in along)
+    terms = [
+        cx * cy * cz, sx * sy * cz, sx * cy * sz, cx * sy * sz,
+        sx * cy * cz, cx * sy * cz, cx * cy * sz, sx * sy * sz,
+    ]
+    return np.stack(terms).astype(np.float32)
 
 
 def np_split(values):
@@ -211,7 +210,7 @@
     return high, low
 
 
-def tables(channels):
+def tables(channels, n, boxes, halves):
     theta = np_theta(TF, TP)
     phi = np_phi(PF, PP)
     eye = np.eye(channels)
@@ -219,16 +218,19 @@
     theta = theta[:, order]
     up_phi = np.kron(np.eye(2), phi.T)
     up_theta = np.kron(theta, eye)
-    down_theta = np.kron(theta.T, eye) * (TF / TP)
     down_phi = np.kron(np.eye(2), phi) * (PF / PP)
     uph, upl = np_split(up_phi)
     uth, utl = np_split(up_theta)
-    dth, dtl = np_split(down_theta)
     dph, dpl = np_split(down_phi)
+    blocks = theta.reshape(n, boxes, halves, TF).transpose(0, 2, 3, 1) * (TF / TP)
+    down = []
+    for block in blocks.reshape(n * halves, TF, boxes):
+        high, low = np_split(np.kron(block, eye))
+        down.append(np.concatenate([high, high, low], axis=1))
     return (
         np.concatenate([uph, uph, upl], axis=0),
         np.concatenate([uth, uth, utl], axis=1),
-        np.concatenate([dth, dth, dtl], axis=1),
+        np.stack(down),
         np.concatenate([dph, dph, dpl], axis=0),
     )
 
@@ -243,118 +245,13 @@
     return jnp.dot(a, b, preferred_element_type=jnp.float32)
 
 
-pair = 2
-
-
-def raise_kernel(slot_ref, x_ref, phi_ref, theta_ref, cos_ref, sin_ref, out_ref):
-    step = pl.program_id(0)
-    channels = x_ref.shape[1]
-    parents = out_ref.shape[1]
-
-    @pl.when(step == 0)
-    def _():
-        out_ref[...] = jnp.zeros_like(out_ref)
-
-    stacked = []
-    for i in range(pair):
-        x = x_ref[i]
-        x = jnp.concatenate(
-            [x[:, j * 2 * PF : (j + 1) * 2 * PF] for j in range(TF // 2)], axis=0
-        )
-        y = dot(split3(x, 1), phi_ref[...])
-        stacked.append(jnp.concatenate([y[:, :PP], y[:, PP:]], axis=0))
-    z = jnp.concatenate(stacked, axis=1)
-    raised = dot(theta_ref[...], split3(z, 0))
-    for i in range(pair):
-        slot = slot_ref[step * pair + i]
-        octant = slot % 8
-        parent = slot // 8 % parents
-        r = raised[:, i * PP : (i + 1) * PP].reshape(TP, channels, PP)
-        turned = pltpu.roll(r, channels // 2, 1)
-        out_ref[:, parent] += r * cos_ref[octant] + turned * sin_ref[octant]
-
-
-def lower_kernel(slot_ref, f_ref, phi_ref, theta_ref, cos_ref, sin_ref, out_ref):
-    step = pl.program_id(0)
-    channels = out_ref.shape[1]
-    parents = f_ref.shape[1]
-    fields = []
-    for i in range(pair):
-        slot = slot_ref[step * pair + i]
-        octant = slot % 8
-        parent = slot // 8 % parents
-        r = f_ref[:, parent]
-        turned = pltpu.roll(r, channels // 2, 1)
-        child = r * cos_ref[octant] - turned * sin_ref[octant]
-        fields.append(child.reshape(TP * channels, PP))
-    z = dot(theta_ref[...], split3(jnp.concatenate(fields, axis=1), 0))
-    half = z.shape[0] // 2
-    for i in range(pair):
-        part = z[:, i * PP : (i + 1) * PP]
-        y = jnp.concatenate([part[:half], part[half:]], axis=1)
-        x = dot(split3(y, 1), phi_ref[...])
-        out_ref[i] = jnp.concatenate(
-            [x[j * channels : (j + 1) * channels] for j in range(TF // 2)], axis=1
-        )
-
-
-def whole_spec(array):
-    return pl.BlockSpec(array.shape, lambda *_: (0,) * array.ndim)
-
-
-def raise_parents(slots, outgoing, parents, consts):
-    fine, channels, width = outgoing.shape
-    phi, theta, cos_table, sin_table = consts
-    shape = (TP, parents, channels, PP)
-    return pl.pallas_call(
-        raise_kernel,
-        out_shape=jax.ShapeDtypeStruct(shape, jnp.float32),
-        grid_spec=pltpu.PrefetchScalarGridSpec(
-            num_scalar_prefetch=1,
-            grid=(fine // pair,),
-            in_specs=[
-                pl.BlockSpec((pair, channels, width), lambda i, _: (i, 0, 0)),
-                whole_spec(phi),
-                whole_spec(theta),
-                whole_spec(cos_table),
-                whole_spec(sin_table),
-            ],
-            out_specs=pl.BlockSpec(shape, lambda i, _: (0, 0, 0, 0)),
-        ),
-        compiler_params=pltpu.CompilerParams(vmem_limit_bytes=48 * 2**20),
-        name="raise_parents",
-    )(slots, outgoing, phi, theta, cos_table, sin_table)
-
-
-def lower_parents(slots, field, consts):
-    parents, channels = field.shape[1:3]
-    fine = slots.shape[0]
-    phi, theta, cos_table, sin_table = consts
-    return pl.pallas_call(
-        lower_kernel,
-        out_shape=jax.ShapeDtypeStruct((fine, channels, TF * PF), jnp.float32),
-        grid_spec=pltpu.PrefetchScalarGridSpec(
-            num_scalar_prefetch=1,
-            grid=(fine // pair,),
-            in_specs=[
-                whole_spec(field),
-                whole_spec(phi),
-                whole_spec(theta),
-                whole_spec(cos_table),
-                whole_spec(sin_table),
-            ],
-            out_specs=pl.BlockSpec((pair, channels, TF * PF), lambda i, _: (i, 0, 0)),
-        ),
-        compiler_params=pltpu.CompilerParams(vmem_limit_bytes=48 * 2**20),
-        name="lower_parents",
-    )(slots, field, phi, theta, cos_table, sin_table)
-
-
 MESH = pl.DeviceIdType.MESH
 
 
 def exchange_kernel(
-    p_ref, partner_ref, kind_ref, rows_ref, out_ref,
+    x_ref, slot_ref, up_phi_ref, up_theta_ref, down_theta_ref, down_phi_ref, phase_ref,
+    partner_ref, kind_ref, count_ref, rows_ref, out_ref,
+    r_ref, turn_ref, own_ref, p_ref, f_ref, child_ref, low_ref,
     sel_ref, op_ref, up_ref, down_ref, band_ref, src_ref, res_ref,
     up_send, up_recv, down_send, down_recv, go_send, go_recv, back_send, back_recv,
     rise_send, rise_recv, sink_send, sink_recv,
@@ -367,6 +264,132 @@
     blocks = sel_ref.shape[0]
     length = partner_ref.shape[1]
     pair_rows = sources * targets
+    fine = x_ref.shape[0]
+    parents = block // channels
+    turn_sign = jnp.where(
+        lax.broadcasted_iota(jnp.int32, (channels, width), 0) < channels // 2, 1.0, -1.0
+    )
+
+    def raise_pair(i, _):
+        stacked = []
+        for f in range(2):
+            x = x_ref[2 * i + f]
+            x = jnp.concatenate(
+                [x[:, j * 2 * PF : (j + 1) * 2 * PF] for j in range(TF // 2)], axis=0
+            )
+            y = dot(split3(x, 1), up_phi_ref[...])
+            stacked.append(jnp.concatenate([y[:, :PP], y[:, PP:]], axis=0))
+        z3 = split3(jnp.concatenate(stacked, axis=1), 0)
+        raised = dot(up_theta_ref[...], z3)
+        r_ref[2 * i] = raised[:, :PP]
+        r_ref[2 * i + 1] = raised[:, PP:]
+        return 0
+
+    def turn_one(f, _):
+        slot = slot_ref[z * fine + f]
+        octant = slot % 8
+        parent = slot // 8 % parents
+        x = (2 * (octant % 2) - 1).astype(jnp.float32)
+        y = (2 * (octant // 2 % 2) - 1).astype(jnp.float32)
+        w = (2 * (octant // 4) - 1).astype(jnp.float32)
+        t = [phase_ref[i] for i in range(8)]
+        turn_ref[f, 0] = t[0] - (x * y) * t[1] - (x * w) * t[2] - (y * w) * t[3]
+        turn_ref[f, 1] = x * t[4] + y * t[5] + w * t[6] - (x * y * w) * t[7]
+        rows = lax.broadcasted_iota(jnp.int32, (parents, width), 0)
+        own_ref[f] = jnp.where(rows == parent, 1.0, 0.0)
+        return 0
+
+    def make_piece(b, h):
+        def one_row(bb, _):
+            u = (b * boxes + bb) * halves + h
+            sums = [jnp.zeros((channels, width), jnp.float32) for _ in range(parents)]
+            for f in range(fine):
+                r = r_ref[f, pl.ds(pl.multiple_of(u * channels, channels), channels), :]
+                cos = turn_ref[f, 0, pl.ds(u, 1), :]
+                sin = turn_ref[f, 1, pl.ds(u, 1), :]
+                moved = r * cos + pltpu.roll(r, channels // 2, 0) * (turn_sign * sin)
+                for p in range(parents):
+                    sums[p] = sums[p] + moved * own_ref[f, p : p + 1, :]
+            for p in range(parents):
+                p_ref[b, bb, h, p * channels : (p + 1) * channels, :] = sums[p]
+            return 0
+
+        lax.fori_loop(0, boxes, one_row, 0)
+
+    def band_at(k):
+        middle = n - 1 - k // 2 if k % 2 == 0 else k // 2
+        return jnp.where(z == 0, n - 1 - k, jnp.where(z == n - 1, k, middle))
+
+    def lower_piece(b, h):
+        def two_rows(i, _):
+            fields = [
+                [
+                    f_ref[b, 2 * i + r, h, p * channels : (p + 1) * channels, :]
+                    for p in range(parents)
+                ]
+                for r in range(2)
+            ]
+            first = (b * boxes + 2 * i) * halves + h
+            for f in range(fine):
+                both = []
+                for r in range(2):
+                    u = first + r * halves
+                    mine = fields[r][0] * own_ref[f, 0:1, :]
+                    for p in range(1, parents):
+                        mine = mine + fields[r][p] * own_ref[f, p : p + 1, :]
+                    cos = turn_ref[f, 0, pl.ds(u, 1), :]
+                    sin = turn_ref[f, 1, pl.ds(u, 1), :]
+                    both.append(
+                        mine * cos - pltpu.roll(mine, channels // 2, 0) * (turn_sign * sin)
+                    )
+                child = jnp.concatenate(both, axis=0)
+                high = child.astype(jnp.bfloat16)
+                low = (child - high.astype(jnp.float32)).astype(jnp.bfloat16)
+                row = pl.multiple_of(i * 2 * channels, 2 * channels)
+                lanes = slice(f * width, (f + 1) * width)
+                child_ref[0, pl.ds(row, 2 * channels), lanes] = high
+                child_ref[1, pl.ds(row, 2 * channels), lanes] = low
+            return 0
+
+        lax.fori_loop(0, boxes // 2, two_rows, 0)
+        tile = 4 * width
+
+        def add_tile(i, _):
+            lanes = pl.ds(pl.multiple_of(i * tile, tile), tile)
+            high = child_ref[0, :, lanes]
+            low = child_ref[1, :, lanes]
+            low_ref[:, lanes] += dot(
+                down_theta_ref[b * halves + h], jnp.concatenate([high, low, high], axis=0)
+            )
+            return 0
+
+        lax.fori_loop(0, fine * width // tile, add_tile, 0)
+
+    def lower_step(h, step):
+        if step == 0:
+            lower_piece(z, h)
+            return
+
+        def one_side(i, _):
+            b = jnp.where(i == 0, z - step, z + step)
+
+            @pl.when((b >= 0) & (b < n))
+            def _():
+                lower_piece(b, h)
+
+            return 0
+
+        lax.fori_loop(0, 2, one_side, 0)
+
+    def lower_last(f, _):
+        part = low_ref[:, pl.ds(pl.multiple_of(f * width, width), width)]
+        half = part.shape[0] // 2
+        y = jnp.concatenate([part[:half], part[half:]], axis=1)
+        x = dot(split3(y, 1), down_phi_ref[...])
+        out_ref[f] = jnp.concatenate(
+            [x[j * channels : (j + 1) * channels] for j in range(TF // 2)], axis=1
+        )
+        return 0
 
     def remote(src, dst, send, recv, to_box, to_dir):
         return pltpu.make_async_remote_copy(
@@ -467,7 +490,7 @@
     def back_copy(h, k):
         return remote(
             res_ref.at[h, pl.ds(pl.multiple_of(peer(k) * block, block), block)],
-            out_ref.at[z, box, h],
+            f_ref.at[z, box, h],
             back_send.at[h, k], back_recv.at[h, k], peer(k), z,
         )
 
@@ -483,18 +506,18 @@
     def back_start(h):
         for k in range(1, boxes):
             back_copy(h, k).start()
-        out_ref[z, box, h] = res_ref[h, pl.ds(pl.multiple_of(box * block, block), block)]
+        f_ref[z, box, h] = res_ref[h, pl.ds(pl.multiple_of(box * block, block), block)]
 
     def back_wait(h):
         for k in range(1, boxes):
             back_copy(h, k).wait_recv()
 
     def rise_copy(h, b):
-        piece = out_ref.at[b, :, h]
+        piece = f_ref.at[b, :, h]
         return remote(piece, piece, rise_send.at[h, b], rise_recv.at[h, b], box, z + 1)
 
     def sink_copy(h, b):
-        piece = out_ref.at[b, :, h]
+        piece = f_ref.at[b, :, h]
         return remote(piece, piece, sink_send.at[h, b], sink_recv.at[h, b], box, z - 1)
 
     def share_step(h, step):
@@ -531,6 +554,8 @@
 
     def count_pairs(p, _):
         partner = partner_ref[pl.ds(p, 1), :]
+        slots = lax.broadcasted_iota(jnp.int32, (1, length), 1)
+        partner = jnp.where(slots < count_ref[p], partner, -1)
         kind = kind_ref[pl.ds(p, 1), :]
         a = jnp.where(source_ids == partner, 1.0, 0.0).astype(jnp.bfloat16)
         b = jnp.where(kind_ids == kind, 1.0, 0.0).astype(jnp.bfloat16)
@@ -613,15 +638,39 @@
         pl.semaphore_signal(barrier, inc=1, device_id=(box, z + 1), device_id_type=MESH)
 
     ends = jnp.where(z > 0, 1, 0) + jnp.where(z < n - 1, 1, 0)
+    lax.fori_loop(0, fine, turn_one, 0)
+    lax.fori_loop(0, fine // 2, raise_pair, 0, unroll=2)
+    low_ref[...] = jnp.zeros_like(low_ref)
+    make_piece(band_at(0), 0)
     pl.semaphore_wait(barrier, boxes - 1 + ends)
-
     sum_send(0)
+    make_piece(band_at(1), 0)
     sum_send(1)
+    for i in range(2, n):
+        make_piece(band_at(i), 0)
+
+    shared = [0] * halves
+    lowered = [0] * halves
+
+    def share_to(h, last_step):
+        while shared[h] <= min(last_step, n - 1):
+            share_step(h, shared[h])
+            shared[h] += 1
+
+    def lower_to(h, last_step):
+        while lowered[h] <= min(last_step, n - 1):
+            lower_step(h, lowered[h])
+            lowered[h] += 1
+
     for h in range(halves):
         tick = h * chunks
         for step in range(1, chunks + 1):
             if h == 0 and step < chunks:
                 count_part(step - 1, chunks - 1)
+                if step == 1:
+                    for later in range(1, halves):
+                        for i in range(n):
+                            make_piece(band_at(i), later)
             if h == 0 and step == chunks:
                 operator_half(h)
             if h and step == 1:
@@ -631,25 +680,36 @@
                 back_start(h - 1)
             if h and step == chunks:
                 back_wait(h - 1)
-                share_step(h - 1, 0)
+                share_to(h - 1, 0)
                 operator_half(h)
             sum_tick(tick + step)
         sum_finish(h)
         go_start(h)
         if h:
-            share_step(h - 1, 1)
+            share_to(h - 1, 1)
+            lower_to(h - 1, 0)
         go_wait(h)
-    apply_half(halves - 1, 0, 2)
-    apply_half(halves - 1, 1, 2)
-    back_start(halves - 1)
-    if halves > 1:
-        share_step(halves - 2, 2)
     last = halves - 1
+    apply_half(last, 0, 2)
+    apply_half(last, 1, 2)
+    back_start(last)
+    for h in range(last):
+        share_to(h, 2)
+        lower_to(h, 1)
     back_wait(last)
-    share_step(last, 0)
-    for h in range(halves):
-        for step in range(3 if h == last - 1 else 1, n):
-            share_step(h, step)
+    share_to(last, 0)
+    for h in range(last):
+        share_to(h, n - 1)
+        lower_to(h, 2)
+    lower_to(last, 0)
+    share_to(last, 1)
+    for h in range(last):
+        lower_to(h, n - 1)
+    lower_to(last, 1)
+    for step in range(2, n):
+        share_to(last, step)
+        lower_to(last, step)
+    lax.fori_loop(0, fine, lower_last, 0, unroll=4)
     for h in range(halves):
         sum_drain(h)
         share_drain(h)
@@ -658,70 +718,69 @@
             back_copy(h, k).wait_send()
 
 
-def exchange(raised, partner, kind, rows, n, boxes, targets):
-    polar, parents, channels, width = raised.shape
-    halves = polar // n // boxes
+def exchange(outgoing, slots, partner, kind, count, rows, n, boxes):
+    fine, channels, fine_width = outgoing.shape
+    parents = slots.shape[0] // 8
+    targets = partner.shape[0]
+    halves = TP // n // boxes
     block = parents * channels
     kinds = rows.shape[0]
     kind_blocks = -(-kinds // 128)
-    shape = (n, boxes, halves, block, width)
+    shape = (n, boxes, halves, block, PP)
     vmem = pl.BlockSpec(memory_space=pltpu.VMEM)
+    smem = pl.BlockSpec(memory_space=pltpu.SMEM)
     dma = pltpu.SemaphoreType.DMA
-    out = pl.pallas_call(
+    consts = [jnp.asarray(t) for t in tables(channels, n, boxes, halves)]
+    f32 = jnp.float32
+    return pl.pallas_call(
         functools.partial(exchange_kernel, targets=targets, channels=channels),
-        out_shape=jax.ShapeDtypeStruct(shape, jnp.float32),
-        in_specs=[vmem] * 4,
+        out_shape=jax.ShapeDtypeStruct(outgoing.shape, f32),
+        in_specs=[vmem, smem] + [vmem] * 7 + [smem, vmem],
         out_specs=vmem,
         scratch_shapes=[
-            pltpu.VMEM((kind_blocks, targets * targets, 128), jnp.float32),
-            pltpu.VMEM((halves, targets * targets, 2 * width), jnp.float32),
-            pltpu.VMEM((halves, n, boxes, block, width), jnp.float32),
-            pltpu.VMEM((halves, n, boxes, block, width), jnp.float32),
-            pltpu.VMEM((halves, boxes, block, width), jnp.float32),
-            pltpu.VMEM((halves, boxes, block, width), jnp.float32),
-            pltpu.VMEM((halves, targets * channels, width), jnp.float32),
+            pltpu.VMEM((fine, TP * channels, PP), f32),
+            pltpu.VMEM((fine, 2, TP, PP), f32),
+            pltpu.VMEM((fine, parents, PP), f32),
+            pltpu.VMEM(shape, f32),
+            pltpu.VMEM(shape, f32),
+            pltpu.VMEM((2, boxes * channels, fine * PP), jnp.bfloat16),
+            pltpu.VMEM((TF * channels, fine * PP), f32),
+            pltpu.VMEM((kind_blocks, targets * targets, 128), f32),
+            pltpu.VMEM((halves, targets * targets, 2 * PP), f32),
+            pltpu.VMEM((halves, n, boxes, block, PP), f32),
+            pltpu.VMEM((halves, n, boxes, block, PP), f32),
+            pltpu.VMEM((halves, boxes, block, PP), f32),
+            pltpu.VMEM((halves, boxes, block, PP), f32),
+            pltpu.VMEM((halves, targets * channels, PP), f32),
         ]
         + [dma((halves, n))] * 4
         + [dma((halves, boxes))] * 4
         + [dma((halves, n))] * 4,
         compiler_params=pltpu.CompilerParams(
-            vmem_limit_bytes=52 * 2**20, collective_id=0, has_side_effects=True
+            vmem_limit_bytes=56 * 2**20, collective_id=0, has_side_effects=True
         ),
         name="exchange",
-    )(raised.reshape(shape), partner, kind, rows)
-    return out.reshape(raised.shape)
+    )(
+        outgoing, slots, *consts, jnp.asarray(np_phase()), partner, kind, count, rows
+    )
 
 
 def body(outgoing, fine_slot, translator, list_partner, list_kind, list_count):
     dir_count = lax.axis_size("dir")
     box_count = lax.axis_size("box")
-    if TP // dir_count % box_count:
+    fine_here, channels, _ = outgoing.shape
+    whole_rows = TP // dir_count % box_count == 0 and dir_count >= 4 and box_count % 2 == 0
+    if not whole_rows or fine_here % 4 or channels % 8 or list_partner.shape[0] % 32:
         return general_body(
             outgoing, fine_slot, translator, list_partner, list_kind, list_count
         )
     box_index = lax.axis_index("box")
-    dir_index = lax.axis_index("dir")
-    fine_here, channels, _ = outgoing.shape
-    parents_here = fine_slot.shape[0] // 8
-    targets, length = list_partner.shape
     kinds, _, dirs_here = translator.shape
     split_here = dirs_here // box_count
-    rows_here = split_here // PP
-
-    up_phi, up_theta, down_theta, down_phi = tables(channels)
-    cos_table, sin_table = (jnp.asarray(t) for t in np_phase(channels))
-    slots = lax.dynamic_slice_in_dim(fine_slot, dir_index * fine_here, fine_here, 0)
-    alive = jnp.arange(length, dtype=jnp.int32)[None, :] < list_count[:, None]
-    partner = jnp.where(alive, list_partner, -1)
     rows = lax.dynamic_slice_in_dim(translator, box_index * split_here, split_here, 2)
     rows = rows.reshape(kinds, 2 * split_here)
-
-    raised = raise_parents(
-        slots, outgoing, parents_here, (jnp.asarray(up_phi), jnp.asarray(up_theta), cos_table, sin_table)
-    )
-    field = exchange(raised, partner, list_kind, rows, dir_count, box_count, targets)
-    return lower_parents(
-        slots, field, (jnp.asarray(down_phi), jnp.asarray(down_theta), cos_table, sin_table)
+    return exchange(
+        outgoing, fine_slot, list_partner, list_kind, list_count, rows, dir_count, box_count
     )
 
 

time: 111 us -> 99 us (0.89)
  Pallas kernels: 104 us -> 94.1 us
    pallas_call x2 -> x0, Pallas kernels: 17.9 us -> none  [the longest x1 9.62 us: lower_parents(): pl.pallas_call(lower_kernel, out_shape=jax.ShapeDtypeStruct((fine, channe...]
    pallas_call x1, Pallas kernels: 86 us -> 94.1 us  [exchange(): pl.pallas_call(functools.partial(exchange_kernel, targets=targets, channe...]
    unnamed x20 -> x3, local copies, waits for them, and re-layouts: 3.22 us -> 3.4 us
where the time goes in v4:
time: 99 us; the launch traced here: 98.8 us
  Pallas kernels  94.1 us (95%)
  local copies, waits for them, and re-layouts  4.71 us (5%)
    pallas_call x1, Pallas kernels, exchange(): pl.pallas_call(functools.partial(exchange_kernel, targets=targets, channe...  94.1 us
    unnamed x3, local copies, waits for them, and re-layouts  3.4 us

profile of v4, /device:TPU:0, one launch (start us, length us, event | category | flops | bytes accessed | tf_op | source)
XLA Modules:
  0.0 98.8 jit_solution(8529755009858096876)
XLA Ops:
  0.0 1.3 %constant_dynamic-slice_fusion = f32[316,2,256]{2,1,0:T(2,128)S(1)} fusion(f32[316,2,2048]{2,1,0:T(2,128)} %param.13, s32[]{:T(128)S(6)} %select_n.3), kind=kLoop, calls=%fused_computation | loop fusion | bytes 1294340 | tf_op jit(solution)/shard_map/dynamic_slice | solution.py:780
  1.3 0.2 pad
  1.5 0.9 copy.12
  2.4 94.1 %exchange.1 = f32[16,8,2048]{2,1,0:T(8,128)} custom-call(f32[16,8,2048]{2,1,0:T(8,128)} %x_ref.1, s32[64]{0:T(128)} %slot_ref.1, bf16[384,256]{1,0:T(8,128)(2,1)} %constant.22.clone.up_phi_ref, bf16[512,768]{1,0:T(8,128)(2,1)} %constant.23.clone.up_theta_ref, bf16[8,256,192]{2,1,0:T(8,128)(2,1)} %constant.24.clone.down_theta_ref, ...), custom_call_target="tpu_custom_call" | custom-call | tf_op jit(solution)/shard_map/exchange/pallas_call | solution.py:735
  96.5 2.3 %copy.14 = f32[16,8,2048]{2,1,0:T(8,128)} copy(f32[16,8,2048]{2,1,0:T(8,128)} %exchange.1) | data formatting | bytes 2097152

commit v5 on v4

--- a/solution.py
+++ b/solution.py
@@ -257,7 +257,8 @@
     rise_send, rise_recv, sink_send, sink_recv,
     *, targets, channels,
 ):
-    n, boxes, halves, block, width = p_ref.shape
+    n, boxes, pieces, block, width = p_ref.shape
+    rows_here = pieces // 2
     box = lax.axis_index("box")
     z = lax.axis_index("dir")
     sources = targets
@@ -265,10 +266,13 @@
     length = partner_ref.shape[1]
     pair_rows = sources * targets
     fine = x_ref.shape[0]
-    parents = block // channels
+    parents = 2 * block // channels
     turn_sign = jnp.where(
         lax.broadcasted_iota(jnp.int32, (channels, width), 0) < channels // 2, 1.0, -1.0
     )
+
+    sublane = lax.broadcasted_iota(jnp.int32, (channels, width), 0)
+    outer = sublane % 4 < 2
 
     def raise_pair(i, _):
         stacked = []
@@ -301,7 +305,7 @@
 
     def make_piece(b, h):
         def one_row(bb, _):
-            u = (b * boxes + bb) * halves + h
+            u = (b * boxes + bb) * rows_here + h
             sums = [jnp.zeros((channels, width), jnp.float32) for _ in range(parents)]
             for f in range(fine):
                 r = r_ref[f, pl.ds(pl.multiple_of(u * channels, channels), channels), :]
@@ -310,8 +314,13 @@
                 moved = r * cos + pltpu.roll(r, channels // 2, 0) * (turn_sign * sin)
                 for p in range(parents):
                     sums[p] = sums[p] + moved * own_ref[f, p : p + 1, :]
-            for p in range(parents):
-                p_ref[b, bb, h, p * channels : (p + 1) * channels, :] = sums[p]
+            for p in range(0, parents, 2):
+                tile = slice(p // 2 * channels, (p // 2 + 1) * channels)
+                one, two = sums[p], sums[p + 1]
+                p_ref[b, bb, 2 * h, tile, :] = jnp.where(outer, one, pltpu.roll(two, 2, 0))
+                p_ref[b, bb, 2 * h + 1, tile, :] = jnp.where(
+                    outer, pltpu.roll(one, channels - 2, 0), two
+                )
             return 0
 
         lax.fori_loop(0, boxes, one_row, 0)
@@ -319,21 +328,28 @@
     def band_at(k):
         middle = n - 1 - k // 2 if k % 2 == 0 else k // 2
         return jnp.where(z == 0, n - 1 - k, jnp.where(z == n - 1, k, middle))
+
+    def by_part(x):
+        later = (sublane >= 4) & (sublane < 6)
+        earlier = (sublane >= 2) & (sublane < 4)
+        return jnp.where(
+            later, pltpu.roll(x, 2, 0), jnp.where(earlier, pltpu.roll(x, channels - 2, 0), x)
+        )
 
     def lower_piece(b, h):
         def two_rows(i, _):
             fields = [
                 [
-                    f_ref[b, 2 * i + r, h, p * channels : (p + 1) * channels, :]
+                    by_part(f_ref[b, 2 * i + r, h, pl.ds(p, channels, stride=parents), :])
                     for p in range(parents)
                 ]
                 for r in range(2)
             ]
-            first = (b * boxes + 2 * i) * halves + h
+            first = (b * boxes + 2 * i) * rows_here + h
             for f in range(fine):
                 both = []
                 for r in range(2):
-                    u = first + r * halves
+                    u = first + r * rows_here
                     mine = fields[r][0] * own_ref[f, 0:1, :]
                     for p in range(1, parents):
                         mine = mine + fields[r][p] * own_ref[f, p : p + 1, :]
@@ -359,7 +375,7 @@
             high = child_ref[0, :, lanes]
             low = child_ref[1, :, lanes]
             low_ref[:, lanes] += dot(
-                down_theta_ref[b * halves + h], jnp.concatenate([high, low, high], axis=0)
+                down_theta_ref[b * rows_here + h], jnp.concatenate([high, low, high], axis=0)
             )
             return 0
 
@@ -404,23 +420,24 @@
         return remote(src, down_ref.at[h, b], down_send.at[h, b], down_recv.at[h, b], box, z - 1)
 
     chunks = n - 1
+    flight = 3
 
     def sum_send(g):
-        if g >= halves * chunks:
+        if g >= pieces * chunks:
             return
         h, j = divmod(g, chunks)
 
         @pl.when(z == 0)
         def _():
-            if g >= 2:
-                h2, j2 = divmod(g - 2, chunks)
+            if g >= flight:
+                h2, j2 = divmod(g - flight, chunks)
                 up_copy(h2, n - 1 - j2, p_ref.at[n - 1 - j2, :, h2]).wait_send()
             up_copy(h, n - 1 - j, p_ref.at[n - 1 - j, :, h]).start()
 
         @pl.when(z == n - 1)
         def _():
-            if g >= 2:
-                h2, j2 = divmod(g - 2, chunks)
+            if g >= flight:
+                h2, j2 = divmod(g - flight, chunks)
                 down_copy(h2, j2, p_ref.at[j2, :, h2]).wait_send()
             down_copy(h, j, p_ref.at[j, :, h]).start()
 
@@ -444,7 +461,7 @@
             down_ref[h, down_b] += p_ref[down_b, :, h]
             copy.start()
 
-        sum_send(tick + 1)
+        sum_send(tick + flight - 1)
 
     def sum_finish(h):
         band_ref[h] = p_ref[z, :, h]
@@ -470,7 +487,7 @@
                 down_copy(h, b, down_ref.at[h, b]).wait_send()
 
         for j in range(chunks):
-            if h * chunks + j >= halves * chunks - 2:
+            if h * chunks + j >= pieces * chunks - flight:
                 @pl.when(z == 0)
                 def _():
                     up_copy(h, n - 1 - j, p_ref.at[n - 1 - j, :, h]).wait_send()
@@ -489,8 +506,8 @@
 
     def back_copy(h, k):
         return remote(
-            res_ref.at[h, pl.ds(pl.multiple_of(peer(k) * block, block), block)],
-            f_ref.at[z, box, h],
+            res_ref.at[h, peer(k)],
+            f_ref.at[z, box, h // 2, pl.ds(h % 2 * block, block)],
             back_send.at[h, k], back_recv.at[h, k], peer(k), z,
         )
 
@@ -506,18 +523,18 @@
     def back_start(h):
         for k in range(1, boxes):
             back_copy(h, k).start()
-        f_ref[z, box, h] = res_ref[h, pl.ds(pl.multiple_of(box * block, block), block)]
+        f_ref[z, box, h // 2, pl.ds(h % 2 * block, block), :] = res_ref[h, box]
 
     def back_wait(h):
         for k in range(1, boxes):
             back_copy(h, k).wait_recv()
 
     def rise_copy(h, b):
-        piece = f_ref.at[b, :, h]
+        piece = f_ref.at[b, :, h // 2, pl.ds(h % 2 * block, block)]
         return remote(piece, piece, rise_send.at[h, b], rise_recv.at[h, b], box, z + 1)
 
     def sink_copy(h, b):
-        piece = f_ref.at[b, :, h]
+        piece = f_ref.at[b, :, h // 2, pl.ds(h % 2 * block, block)]
         return remote(piece, piece, sink_send.at[h, b], sink_recv.at[h, b], box, z - 1)
 
     def share_step(h, step):
@@ -570,9 +587,9 @@
         first, last = targets * part // parts, targets * (part + 1) // parts
         lax.fori_loop(first, last, count_pairs, 0, unroll=4)
 
-    def operator_half(h):
+    def operator_part(h, part, parts):
         rows = jnp.concatenate(
-            [rows_ref[:, i * width : (i + 1) * width] for i in (h, halves + h)], axis=1
+            [rows_ref[:, i * width : (i + 1) * width] for i in (h, rows_here + h)], axis=1
         )
         pad = blocks * 128 - rows.shape[0]
         if pad:
@@ -592,38 +609,40 @@
             )
             return 0
 
-        lax.fori_loop(0, pair_rows // tile, one_tile, 0)
-
-    def apply_half(h, part, parts):
-        half = channels // 2
-        group = 2
-        per_box = block // channels
-
-        def add_source(s, sums, first):
-            giver = s // per_box
-            row0 = (s % per_box) * channels
-            fields = [src_ref[h, giver, pl.ds(row0 + c, 1), :] for c in range(channels)]
-            out = []
-            for g in range(group):
-                row = pl.multiple_of(s * targets + first + g * 8, 8)
-                real = op_ref[h, pl.ds(row, 8), 0:width]
-                imag = op_ref[h, pl.ds(row, 8), width : 2 * width]
-                mine = sums[g * channels : (g + 1) * channels]
-                for e in range(half):
-                    out.append(mine[e] + real * fields[e] - imag * fields[half + e])
-                for e in range(half):
-                    out.append(mine[half + e] + real * fields[half + e] + imag * fields[e])
-            return tuple(out)
-
-        for first in range(targets * part // parts, targets * (part + 1) // parts, group * 8):
-            sums = tuple(jnp.zeros((8, width), jnp.float32) for _ in range(group * channels))
+        tiles = pair_rows // tile
+        lax.fori_loop(tiles * part // parts, tiles * (part + 1) // parts, one_tile, 0)
+
+    def apply_piece(h):
+        group = 4
+        pairs = parents // 2
+
+        def add_sources(i, sums, first):
+            tile = i % pairs * channels
+            for two in range(2):
+                real_rows = [tile + two * 2 + j for j in range(2)]
+                reals = [src_ref[h, i // pairs, pl.ds(r, 1), :] for r in real_rows]
+                imags = [src_ref[h, i // pairs, pl.ds(r + 4, 1), :] for r in real_rows]
+                out = []
+                for g in range(group):
+                    row = pl.multiple_of((2 * i + two) * targets + first + g * 8, 8)
+                    real = op_ref[h // 2, pl.ds(row, 8), 0:width]
+                    imag = op_ref[h // 2, pl.ds(row, 8), width : 2 * width]
+                    mine = sums[g * 4 : (g + 1) * 4]
+                    for j in range(2):
+                        out.append(mine[j] + real * reals[j] - imag * imags[j])
+                    for j in range(2):
+                        out.append(mine[2 + j] + real * imags[j] + imag * reals[j])
+                sums = tuple(out)
+            return sums
+
+        for first in range(0, targets, group * 8):
+            sums = tuple(jnp.zeros((8, width), jnp.float32) for _ in range(group * 4))
             sums = lax.fori_loop(
-                0, sources, functools.partial(add_source, first=first), sums, unroll=4
+                0, sources // 2, functools.partial(add_sources, first=first), sums, unroll=2
             )
             for g in range(group):
-                for c in range(channels):
-                    start = (first + g * 8) * channels + c
-                    res_ref[h, pl.ds(start, 8, stride=channels), :] = sums[g * channels + c]
+                for c in range(4):
+                    res_ref[h, first // 8 + g, c * 8 : (c + 1) * 8, :] = sums[g * 4 + c]
 
     barrier = pltpu.get_barrier_semaphore()
     for k in range(1, boxes):
@@ -644,73 +663,93 @@
     make_piece(band_at(0), 0)
     pl.semaphore_wait(barrier, boxes - 1 + ends)
     sum_send(0)
-    make_piece(band_at(1), 0)
-    sum_send(1)
-    for i in range(2, n):
+    for i in range(1, n):
         make_piece(band_at(i), 0)
-
-    shared = [0] * halves
-    lowered = [0] * halves
+        if i < flight:
+            sum_send(i)
+
+    shared = [0] * pieces
+    lowered = [0] * rows_here
 
     def share_to(h, last_step):
-        while shared[h] <= min(last_step, n - 1):
+        while h < pieces and shared[h] <= min(last_step, n - 1):
             share_step(h, shared[h])
             shared[h] += 1
 
-    def lower_to(h, last_step):
-        while lowered[h] <= min(last_step, n - 1):
-            lower_step(h, lowered[h])
-            lowered[h] += 1
-
-    for h in range(halves):
-        tick = h * chunks
+    def lower_to(row, last_step):
+        while lowered[row] <= min(last_step, n - 1):
+            lower_step(row, lowered[row])
+            lowered[row] += 1
+
+    def apply_next(h):
+        go_wait(h)
+        apply_piece(h)
+        back_start(h)
+
+    for h in range(pieces):
         for step in range(1, chunks + 1):
-            if h == 0 and step < chunks:
-                count_part(step - 1, chunks - 1)
-                if step == 1:
-                    for later in range(1, halves):
-                        for i in range(n):
-                            make_piece(band_at(i), later)
-            if h == 0 and step == chunks:
-                operator_half(h)
-            if h and step == 1:
-                apply_half(h - 1, 0, 2)
-            if h and step == 2:
-                apply_half(h - 1, 1, 2)
-                back_start(h - 1)
-            if h and step == chunks:
-                back_wait(h - 1)
-                share_to(h - 1, 0)
-                operator_half(h)
-            sum_tick(tick + step)
+            if h == 0:
+                count_part(step - 1, chunks)
+            elif h == 1 and step == 1:
+                for row in range(1, rows_here):
+                    for i in range(n):
+                        make_piece(band_at(i), row)
+            elif h == 1 and step == 2:
+                operator_part(0, 0, 1)
+            elif h == 1 and step == chunks:
+                apply_next(0)
+            elif h >= 2 and step == 1:
+                if h % 2 == 0:
+                    operator_part(h // 2, 0, 2)
+                else:
+                    share_to(h - 3, 2)
+                    apply_next(h - 1)
+                    share_to(h - 2, 1)
+            elif h >= 2 and step == 2:
+                if h % 2 == 0:
+                    apply_next(h - 1)
+                    back_wait(h - 2)
+                    share_to(h - 2, 0)
+                else:
+                    share_to(h - 3, n - 1)
+                    back_wait(h - 1)
+                    share_to(h - 1, 0)
+            elif h >= 2 and step == chunks:
+                if h % 2 == 0:
+                    operator_part(h // 2, 1, 2)
+                    back_wait(h - 1)
+                    share_to(h - 1, 0)
+                    share_to(h - 2, 1)
+                else:
+                    share_to(h - 2, 2)
+                    lower_to(h // 2 - 1, 0)
+            sum_tick(h * chunks + step)
         sum_finish(h)
         go_start(h)
-        if h:
-            share_to(h - 1, 1)
-            lower_to(h - 1, 0)
-        go_wait(h)
-    last = halves - 1
-    apply_half(last, 0, 2)
-    apply_half(last, 1, 2)
-    back_start(last)
-    for h in range(last):
-        share_to(h, 2)
-        lower_to(h, 1)
+    last = pieces - 1
+    share_to(last - 1, 1)
+    apply_next(last)
+    for h in range(last - 1):
+        share_to(h, n - 1)
+    share_to(last - 1, 2)
     back_wait(last)
     share_to(last, 0)
-    for h in range(last):
-        share_to(h, n - 1)
-        lower_to(h, 2)
-    lower_to(last, 0)
+    for row in range(rows_here - 1):
+        lower_to(row, 1)
+    share_to(last - 1, n - 1)
     share_to(last, 1)
-    for h in range(last):
-        lower_to(h, n - 1)
-    lower_to(last, 1)
+    for row in range(rows_here - 1):
+        lower_to(row, 2)
+    lower_to(rows_here - 1, 0)
+    share_to(last, 2)
+    for row in range(rows_here - 1):
+        lower_to(row, n - 1)
+    lower_to(rows_here - 1, 1)
     for step in range(2, n):
         share_to(last, step)
-        lower_to(last, step)
+        lower_to(rows_here - 1, step)
     lax.fori_loop(0, fine, lower_last, 0, unroll=4)
-    for h in range(halves):
+    for h in range(pieces):
         sum_drain(h)
         share_drain(h)
         for k in range(1, boxes):
@@ -723,10 +762,11 @@
     parents = slots.shape[0] // 8
     targets = partner.shape[0]
     halves = TP // n // boxes
-    block = parents * channels
+    pieces = 2 * halves
+    block = parents * channels // 2
     kinds = rows.shape[0]
     kind_blocks = -(-kinds // 128)
-    shape = (n, boxes, halves, block, PP)
+    shape = (n, boxes, pieces, block, PP)
     vmem = pl.BlockSpec(memory_space=pltpu.VMEM)
     smem = pl.BlockSpec(memory_space=pltpu.SMEM)
     dma = pltpu.SemaphoreType.DMA
@@ -742,20 +782,20 @@
             pltpu.VMEM((fine, 2, TP, PP), f32),
             pltpu.VMEM((fine, parents, PP), f32),
             pltpu.VMEM(shape, f32),
-            pltpu.VMEM(shape, f32),
+            pltpu.VMEM((n, boxes, halves, 2 * block, PP), f32),
             pltpu.VMEM((2, boxes * channels, fine * PP), jnp.bfloat16),
             pltpu.VMEM((TF * channels, fine * PP), f32),
             pltpu.VMEM((kind_blocks, targets * targets, 128), f32),
             pltpu.VMEM((halves, targets * targets, 2 * PP), f32),
-            pltpu.VMEM((halves, n, boxes, block, PP), f32),
-            pltpu.VMEM((halves, n, boxes, block, PP), f32),
-            pltpu.VMEM((halves, boxes, block, PP), f32),
-            pltpu.VMEM((halves, boxes, block, PP), f32),
-            pltpu.VMEM((halves, targets * channels, PP), f32),
+            pltpu.VMEM((pieces, n, boxes, block, PP), f32),
+            pltpu.VMEM((pieces, n, boxes, block, PP), f32),
+            pltpu.VMEM((pieces, boxes, block, PP), f32),
+            pltpu.VMEM((pieces, boxes, block, PP), f32),
+            pltpu.VMEM((pieces, boxes, block, PP), f32),
         ]
-        + [dma((halves, n))] * 4
-        + [dma((halves, boxes))] * 4
-        + [dma((halves, n))] * 4,
+        + [dma((pieces, n))] * 4
+        + [dma((pieces, boxes))] * 4
+        + [dma((pieces, n))] * 4,
         compiler_params=pltpu.CompilerParams(
             vmem_limit_bytes=56 * 2**20, collective_id=0, has_side_effects=True
         ),
@@ -770,7 +810,7 @@
     box_count = lax.axis_size("box")
     fine_here, channels, _ = outgoing.shape
     whole_rows = TP // dir_count % box_count == 0 and dir_count >= 4 and box_count % 2 == 0
-    if not whole_rows or fine_here % 4 or channels % 8 or list_partner.shape[0] % 32:
+    if not whole_rows or fine_here % 4 or channels != 8 or fine_slot.shape[0] != 64 or list_partner.shape[0] % 32:
         return general_body(
             outgoing, fine_slot, translator, list_partner, list_kind, list_count
         )

time: 99 us -> 100 us (1.010)
  Pallas kernels: 94.1 us -> 95.4 us
    pallas_call x1, Pallas kernels: 94.1 us -> 95.4 us  [exchange(): pl.pallas_call(functools.partial(exchange_kernel, targets=targets, channe...]
where the time goes in v5:
time: 100 us
  Pallas kernels  95.4 us (95%)
  local copies, waits for them, and re-layouts  4.71 us (5%)
    pallas_call x1, Pallas kernels, exchange(): pl.pallas_call(functools.partial(exchange_kernel, targets=targets, channe...  95.4 us
    unnamed x3, local copies, waits for them, and re-layouts  3.4 us

profile of v5, /device:TPU:0, one launch (start us, length us, event | category | flops | bytes accessed | tf_op | source)
XLA Modules:
  0.0 100.1 jit_solution(10921735786828532658)
XLA Ops:
  0.0 1.3 %constant_dynamic-slice_fusion = f32[316,2,256]{2,1,0:T(2,128)S(1)} fusion(f32[316,2,2048]{2,1,0:T(2,128)} %param.13, s32[]{:T(128)S(6)} %select_n.3), kind=kLoop, calls=%fused_computation | loop fusion | bytes 1294340 | tf_op jit(solution)/shard_map/dynamic_slice | solution.py:820
  1.3 0.2 pad
  1.5 0.9 copy.12
  2.4 95.4 %exchange.1 = f32[16,8,2048]{2,1,0:T(8,128)} custom-call(f32[16,8,2048]{2,1,0:T(8,128)} %x_ref.1, s32[64]{0:T(128)} %slot_ref.1, bf16[384,256]{1,0:T(8,128)(2,1)} %constant.22.clone.up_phi_ref, bf16[512,768]{1,0:T(8,128)(2,1)} %constant.23.clone.up_theta_ref, bf16[8,256,192]{2,1,0:T(8,128)(2,1)} %constant.24.clone.down_theta_ref, ...), custom_call_target="tpu_custom_call" | custom-call | tf_op jit(solution)/shard_map/exchange/pallas_call | solution.py:775
  97.8 2.3 %copy.14 = f32[16,8,2048]{2,1,0:T(8,128)} copy(f32[16,8,2048]{2,1,0:T(8,128)} %exchange.1) | data formatting | bytes 2097152

commit v6 on v5

--- a/solution.py
+++ b/solution.py
@@ -686,54 +686,52 @@
         apply_piece(h)
         back_start(h)
 
+    def go_back(h):
+        back_wait(h)
+        share_to(h, 0)
+
     for h in range(pieces):
         for step in range(1, chunks + 1):
             if h == 0:
                 count_part(step - 1, chunks)
-            elif h == 1 and step == 1:
-                for row in range(1, rows_here):
-                    for i in range(n):
-                        make_piece(band_at(i), row)
-            elif h == 1 and step == 2:
-                operator_part(0, 0, 1)
-            elif h == 1 and step == chunks:
-                apply_next(0)
-            elif h >= 2 and step == 1:
-                if h % 2 == 0:
-                    operator_part(h // 2, 0, 2)
+            elif step == 1:
+                if h == 1:
+                    for row in range(1, rows_here):
+                        for i in range(n):
+                            make_piece(band_at(i), row)
                 else:
-                    share_to(h - 3, 2)
+                    if h % 2 == 0:
+                        operator_part(h // 2, 1, 2)
+                    else:
+                        share_to(h - 3, 2)
+                        share_to(h - 2, 1)
                     apply_next(h - 1)
-                    share_to(h - 2, 1)
-            elif h >= 2 and step == 2:
-                if h % 2 == 0:
-                    apply_next(h - 1)
-                    back_wait(h - 2)
-                    share_to(h - 2, 0)
+            elif step == 2:
+                if h == 1:
+                    operator_part(0, 0, 1)
+                    apply_next(0)
                 else:
-                    share_to(h - 3, n - 1)
-                    back_wait(h - 1)
-                    share_to(h - 1, 0)
-            elif h >= 2 and step == chunks:
-                if h % 2 == 0:
-                    operator_part(h // 2, 1, 2)
-                    back_wait(h - 1)
-                    share_to(h - 1, 0)
-                    share_to(h - 2, 1)
-                else:
+                    go_back(h - 1)
+                    share_to(h - 2 if h % 2 == 0 else h - 3, n - 1 if h % 2 else 1)
+            elif step == chunks:
+                if h == 1:
+                    go_back(0)
+                if h % 2 and h + 1 < pieces:
+                    operator_part(h // 2 + 1, 0, 2)
+                if h % 2 and h > 1:
                     share_to(h - 2, 2)
-                    lower_to(h // 2 - 1, 0)
+                    share_to(h - 1, 1)
             sum_tick(h * chunks + step)
         sum_finish(h)
         go_start(h)
     last = pieces - 1
-    share_to(last - 1, 1)
-    apply_next(last)
     for h in range(last - 1):
         share_to(h, n - 1)
+    apply_next(last)
     share_to(last - 1, 2)
-    back_wait(last)
-    share_to(last, 0)
+    for row in range(rows_here - 1):
+        lower_to(row, 0)
+    go_back(last)
     for row in range(rows_here - 1):
         lower_to(row, 1)
     share_to(last - 1, n - 1)

time: 100 us -> 104 us (1.040)
  Pallas kernels: 95.4 us -> 98.7 us
    pallas_call x1, Pallas kernels: 95.4 us -> 98.7 us  [exchange(): pl.pallas_call(functools.partial(exchange_kernel, targets=targets, channe...]
where the time goes in v6:
time: 104 us; the launch traced here: 103 us
  Pallas kernels  98.7 us (95%)
  local copies, waits for them, and re-layouts  4.71 us (5%)
    pallas_call x1, Pallas kernels, exchange(): pl.pallas_call(functools.partial(exchange_kernel, targets=targets, channe...  98.7 us
    unnamed x3, local copies, waits for them, and re-layouts  3.4 us

profile of v6, /device:TPU:0, one launch (start us, length us, event | category | flops | bytes accessed | tf_op | source)
XLA Modules:
  0.0 103.5 jit_solution(15538844669902851399)
XLA Ops:
  0.0 1.3 %constant_dynamic-slice_fusion = f32[316,2,256]{2,1,0:T(2,128)S(1)} fusion(f32[316,2,2048]{2,1,0:T(2,128)} %param.13, s32[]{:T(128)S(6)} %select_n.3), kind=kLoop, calls=%fused_computation | loop fusion | bytes 1294340 | tf_op jit(solution)/shard_map/dynamic_slice | solution.py:818
  1.3 0.2 pad
  1.5 0.9 copy.12
  2.4 98.7 %exchange.1 = f32[16,8,2048]{2,1,0:T(8,128)} custom-call(f32[16,8,2048]{2,1,0:T(8,128)} %x_ref.1, s32[64]{0:T(128)} %slot_ref.1, bf16[384,256]{1,0:T(8,128)(2,1)} %constant.22.clone.up_phi_ref, bf16[512,768]{1,0:T(8,128)(2,1)} %constant.23.clone.up_theta_ref, bf16[8,256,192]{2,1,0:T(8,128)(2,1)} %constant.24.clone.down_theta_ref, ...), custom_call_target="tpu_custom_call" | custom-call | tf_op jit(solution)/shard_map/exchange/pallas_call | solution.py:773
  101.2 2.3 %copy.14 = f32[16,8,2048]{2,1,0:T(8,128)} copy(f32[16,8,2048]{2,1,0:T(8,128)} %exchange.1) | data formatting | bytes 2097152

commit v7 on v4

--- a/solution.py
+++ b/solution.py
@@ -675,10 +675,9 @@
                 operator_half(h)
             if h and step == 1:
                 apply_half(h - 1, 0, 2)
-            if h and step == 2:
                 apply_half(h - 1, 1, 2)
                 back_start(h - 1)
-            if h and step == chunks:
+            if h and step == 2:
                 back_wait(h - 1)
                 share_to(h - 1, 0)
                 operator_half(h)

time: 99 us -> 103 us (1.040)
  Pallas kernels: 94.1 us -> 97.6 us
    pallas_call x1, Pallas kernels: 94.1 us -> 97.6 us  [exchange(): pl.pallas_call(functools.partial(exchange_kernel, targets=targets, channe...]
where the time goes in v7:
time: 103 us; the launch traced here: 102 us
  Pallas kernels  97.6 us (95%)
  local copies, waits for them, and re-layouts  4.71 us (5%)
    pallas_call x1, Pallas kernels, exchange(): pl.pallas_call(functools.partial(exchange_kernel, targets=targets, channe...  97.6 us
    unnamed x3, local copies, waits for them, and re-layouts  3.4 us

profile of v7, /device:TPU:0, one launch (start us, length us, event | category | flops | bytes accessed | tf_op | source)
XLA Modules:
  0.0 102.3 jit_solution(729734514189643066)
XLA Ops:
  0.0 1.3 %constant_dynamic-slice_fusion = f32[316,2,256]{2,1,0:T(2,128)S(1)} fusion(f32[316,2,2048]{2,1,0:T(2,128)} %param.13, s32[]{:T(128)S(6)} %select_n.3), kind=kLoop, calls=%fused_computation | loop fusion | bytes 1294340 | tf_op jit(solution)/shard_map/dynamic_slice | solution.py:779
  1.3 0.2 pad
  1.5 0.9 copy.12
  2.4 97.6 %exchange.1 = f32[16,8,2048]{2,1,0:T(8,128)} custom-call(f32[16,8,2048]{2,1,0:T(8,128)} %x_ref.1, s32[64]{0:T(128)} %slot_ref.1, bf16[384,256]{1,0:T(8,128)(2,1)} %constant.22.clone.up_phi_ref, bf16[512,768]{1,0:T(8,128)(2,1)} %constant.23.clone.up_theta_ref, bf16[8,256,192]{2,1,0:T(8,128)(2,1)} %constant.24.clone.down_theta_ref, ...), custom_call_target="tpu_custom_call" | custom-call | tf_op jit(solution)/shard_map/exchange/pallas_call | solution.py:734
  100.0 2.3 %copy.14 = f32[16,8,2048]{2,1,0:T(8,128)} copy(f32[16,8,2048]{2,1,0:T(8,128)} %exchange.1) | data formatting | bytes 2097152
